TPU v7x, 256 devices: a whole 4x4x8 slice. The times are simulated.
256 devices in a mesh: clusters: 4 (over x_lo, core), members: 64 (over x_hi, z, y).
Axes of the slice: x: 4 (x_hi: 2, x_lo: 2; x = x_hi * 2 + x_lo), y: 4, z: 8, core: 2. Of those that a mesh axis runs over, the one named last changes fastest.
Arguments:
- embeddings: bfloat16 [65536, 768], P(('clusters', 'members')), parts along dimension 0, may hold values from -400 to 400
- ranks: int32 [65536], P(('clusters', 'members')), parts along dimension 0, may hold values from 0 to 16383, as said below
Outputs:
- max_similarity: float32 [65536], P(('clusters', 'members')), parts along dimension 0
There are 4 independent parts, one for each index of `clusters`. A program takes and returns all parts, laid end to end along the dimension named above; each array names one. Nothing has to cross between parts.
Inputs may be any that keep to these rules, and one draw needn't show every extreme that they name: The rows 256 * b to 256 * (b + 1) - 1 hold the ranks 256 * b to 256 * (b + 1) - 1, each once, in some order.
All inputs are finite; a program needn't handle non-finite values.
Results may differ from a plain program's by a relative error of at most 0.00053.
Values may be sent and summed in bfloat16 or wider, within the bound.
No kernel may reach another device: no remote copies, remote signals or barrier semaphores. Data moves between devices by JAX's collectives and lax.ppermute only.
A program may use at most 64 MiB of HBM per device.

v0:
```python
import jax
import jax.numpy as jnp
from jax import lax
from jax.experimental import pallas as pl
from jax.experimental.pallas import tpu as pltpu
from jax.sharding import PartitionSpec as P

SIZES = (2, 8, 4)
SENDS = [((0,), (0, 2, 0)), ((0,), (1, 0, 1)), ((0,), (0, 0, -1)), ((0,), (0, 0, 1)), ((0,), (0, 1, 0)), ((1,), (0, 1, 0)), ((4,), (0, 0, 1)), ((3,), (1, 0, 0)), ((2,), (0, 0, 1)), ((2,), (0, 0, -1)), ((6,), (0, 1, 0))]
ROWS = [5, 1, 6]
STAGES = [[(1, 0), (2, 0), (2, 1), (3, 0), (3, 1), (3, 2), (4, 1), (4, 2), (4, 3), (5, 0), (5, 2), (5, 3), (5, 4)], [(6, 0), (6, 2), (6, 3), (6, 4), (7, 1), (7, 5), (7, 6), (8, 1), (8, 5), (8, 6)], [(11, 0), (11, 2), (11, 3), (11, 4), (11, 7), (11, 8), (11, 9), (11, 10), (9, 1), (9, 5), (9, 6), (10, 1), (10, 5), (10, 6)]]
FIRST = 6
HELD = (1,)
BOTH = ("clusters", "members")


def member(coords):
    x, z, y = coords
    return ((x % SIZES[0]) * SIZES[1] + z % SIZES[1]) * SIZES[2] + y % SIZES[2]


def coords_of(index):
    return index // (SIZES[1] * SIZES[2]), (index // SIZES[2]) % SIZES[1], index % SIZES[2]


def mirrored(cluster, shift):
    sign = 1 - 2 * (cluster % 2)
    return shift[0], sign * shift[1], sign * shift[2]


def moved(index, cluster, shift):
    return member(tuple(a + b for a, b in zip(coords_of(index), mirrored(cluster, shift))))


def layout():
    places, homes = [(0, 0, 0)], [(0, 0)]
    for number, (slots, shift) in enumerate(SENDS):
        for place, slot in enumerate(slots):
            places.append(tuple(a + b for a, b in zip(places[slot], shift)))
            homes.append((number + 1, place))
    return places, homes


def shift_pairs(shift, back, clusters, members):
    out = []
    for cluster in range(clusters):
        for index in range(members):
            other = cluster * members + moved(index, cluster, shift)
            here = cluster * members + index
            out.append((here, other) if back else (other, here))
    return out


def normalize_kernel(x_ref, out_ref):
    values = x_ref[...].astype(jnp.float32)
    scale = lax.rsqrt(jnp.sum(values * values, axis=1, keepdims=True) + 1e-06)
    out_ref[...] = (values * scale).astype(jnp.bfloat16)


def normalize(embeddings):
    return pl.pallas_call(
        normalize_kernel,
        out_shape=jax.ShapeDtypeStruct(embeddings.shape, jnp.bfloat16),
        in_specs=[pl.BlockSpec(memory_space=pltpu.VMEM)],
        out_specs=pl.BlockSpec(memory_space=pltpu.VMEM),
        compiler_params=pltpu.CompilerParams(vmem_limit_bytes=32 << 20),
        cost_estimate=pl.CostEstimate(flops=4 * embeddings.size, bytes_accessed=4 * embeddings.size, transcendentals=0),
    )(embeddings)


def gather_kernel(found_ref, *refs):
    best = jnp.max(found_ref[...], axis=0)
    for ref in refs[:-1]:
        best = jnp.maximum(best, ref[...])
    refs[-1][...] = best


def plane_groups(members):
    groups = [[m for m in range(members) if coords_of(m)[1] == z] for z in range(SIZES[1])]
    return groups


def place_in_group(member_index):
    plane = SIZES[1] * SIZES[2]
    return lax.div(member_index, plane) * SIZES[2] + lax.rem(member_index, SIZES[2])


def products(a, b):
    return lax.dot_general(a, b, (((1,), (1,)), ((), ())), preferred_element_type=jnp.float32)


def fold(scores):
    rows, columns = scores.shape
    return jnp.max(scores.reshape(rows // 8, 8, columns), axis=0)


def own_kernel(unit_ref, column_ref, row_ref, best_ref):
    best_ref[...] = jnp.full_like(best_ref, -1.0)
    earlier = column_ref[...] < row_ref[...]
    scores = products(unit_ref[...], unit_ref[...])
    best_ref[0] = fold(jnp.where(earlier, scores, jnp.float32(-1.0)))


def stage_kernel(slots, pairs, last, *refs):
    count = len(slots)
    order_ref, blocks, before_ref = refs[0], refs[1 : 1 + count], refs[1 + count]
    *outs, best = refs[2 + count :]
    out = outs[0]
    best[...] = before_ref[...]
    for a, b in pairs:
        higher = order_ref[a] > order_ref[b]
        scores = products(blocks[slots.index(a)][...], blocks[slots.index(b)][...])
        best[b] = jnp.where(higher, best[b], jnp.maximum(best[b], fold(scores)))
        best[a] = jnp.where(higher, jnp.maximum(best[a], jnp.max(scores, axis=1)[None, :]), best[a])
    if last:
        out[...] = jnp.full_like(out, -1.0)
        places = layout()[0]
        for slot in range(best.shape[0]):
            row = jnp.max(best[slot], axis=0, keepdims=True)
            if places[slot][1] == 0:
                out[place_in_group(order_ref[slot])] = row
            elif slot in ROWS:
                outs[1 + ROWS.index(slot)][...] = row
    else:
        out[...] = best[...]


def call_kernel(kernel, shapes, specs, scratch, products_done, *args):
    rows, width = 256, 768
    return pl.pallas_call(
        kernel,
        out_shape=[jax.ShapeDtypeStruct(one, jnp.float32) for one in shapes],
        in_specs=specs,
        out_specs=[pl.BlockSpec(memory_space=pltpu.VMEM)] * len(shapes),
        scratch_shapes=scratch,
        compiler_params=pltpu.CompilerParams(vmem_limit_bytes=32 << 20),
        cost_estimate=pl.CostEstimate(
            flops=2 * rows * rows * width * products_done,
            bytes_accessed=2 * rows * width * products_done,
            transcendentals=0,
        ),
    )(*args)


def per_device(clusters, members, embeddings, ranks):
    cluster, index = lax.axis_index("clusters"), lax.axis_index("members")
    places, _ = layout()
    order = jnp.stack([moved(index, cluster, place) for place in places])
    rows = embeddings.shape[0]
    total = len(places)
    plane = members // SIZES[1]
    smem = pl.BlockSpec(memory_space=pltpu.SMEM)
    vmem = pl.BlockSpec(memory_space=pltpu.VMEM)
    blocks = [embeddings]
    units = {0: normalize(embeddings)}
    (best,) = call_kernel(
        own_kernel, [(total, 8, rows)], [vmem] * 3, [], 1, units[0], ranks.reshape(rows, 1), ranks.reshape(1, rows)
    )

    def compare(stage, best):
        pairs, last = STAGES[stage], stage == len(STAGES) - 1
        slots = sorted({s for pair in pairs for s in pair})
        new = [slot for slot in slots if slot not in units]
        *raw, best = lax.optimization_barrier((*[blocks[slot] for slot in new], best))
        units.update({slot: normalize(block) for slot, block in zip(new, raw)})

        def kernel(*refs):
            stage_kernel(slots, pairs, last, *refs)

        return call_kernel(
            kernel,
            [(plane, 1, rows)] + [(1, rows)] * len(ROWS) if last else [(total, 8, rows)],
            [smem] + [vmem] * (len(slots) + 1),
            [pltpu.VMEM((total, 8, rows), jnp.float32)],
            len(pairs),
            order,
            *[units[s] for s in slots],
            best,
        )

    held = list(HELD)
    for (slot,), shift in SENDS:
        if slot and len(blocks) == FIRST:
            early = held.pop(0)
            blocks[early], best, order = lax.optimization_barrier((blocks[early], best, order))
        if slot in held:
            held.remove(slot)
            (best,) = compare(0, best)
            blocks[slot], best = lax.optimization_barrier((blocks[slot], best))
        blocks.append(lax.ppermute(blocks[slot], BOTH, shift_pairs(shift, False, clusters, members)))
    for stage in range(len(HELD) - 1, len(STAGES)):
        best, *rest = compare(stage, best)
    backs = [
        lax.ppermute(row, BOTH, shift_pairs(places[slot], True, clusters, members))
        for row, slot in zip(rest, ROWS)
    ]
    found = lax.all_to_all(best, "members", 0, 0, axis_index_groups=plane_groups(members), tiled=True)
    (result,) = call_kernel(gather_kernel, [(1, rows)], [vmem] * (1 + len(ROWS)), [], 0, found, *backs)
    return result[0]


def solution(mesh):
    clusters, members = mesh.shape["clusters"], mesh.shape["members"]
    in_specs = (P(BOTH, None), P(BOTH))

    def body(embeddings, ranks):
        return per_device(clusters, members, embeddings, ranks)

    return jax.shard_map(body, mesh=mesh, in_specs=in_specs, out_specs=P(BOTH), check_vma=False)
```

profile of v0, /device:TPU:38, one launch (start us, length us, event | category | flops | bytes accessed | tf_op | source)
XLA Modules:
  0.0 59.3 jit_solution(16636435260036637681)
XLA Ops:
  0.0 0.0 copy-start
  0.0 5.4 %collective-permute-start = (bf16[256,768]{1,0:T(8,128)(2,1)}, bf16[256,768]{1,0:T(8,128)(2,1)S(1)}, u32[]{:S(2)}, u32[]{:S(2)}) collective-permute-start(bf16[256,768]{1,0:T(8,128)(2,1)} %x_ref.1), channel_id=1, source_target_pairs={{8,0},{9,1},{10,2},{11,3},{12,4},{13,5},{14,6},{15,7},{16,8},{17,9... | collective-permute-start | bytes 1179656 | tf_op jit(solution)/shard_map/ppermute | solution.py:190
  5.4 1.6 %collective-permute-start.2 = (bf16[256,768]{1,0:T(8,128)(2,1)}, bf16[256,768]{1,0:T(8,128)(2,1)S(1)}, u32[]{:S(2)}, u32[]{:S(2)}) collective-permute-start(bf16[256,768]{1,0:T(8,128)(2,1)} %x_ref.1), channel_id=1, source_target_pairs={{3,0},{0,1},{1,2},{2,3},{7,4},{4,5},{5,6},{6,7},{11,8},{8,9},{9,10... | collective-permute-start | bytes 1179656 | tf_op jit(solution)/shard_map/ppermute | solution.py:190
  7.0 1.7 %collective-permute-start.3 = (bf16[256,768]{1,0:T(8,128)(2,1)}, bf16[256,768]{1,0:T(8,128)(2,1)S(1)}, u32[]{:S(2)}, u32[]{:S(2)}) collective-permute-start(bf16[256,768]{1,0:T(8,128)(2,1)} %x_ref.1), channel_id=1, source_target_pairs={{1,0},{2,1},{3,2},{0,3},{5,4},{6,5},{7,6},{4,7},{9,8},{10,9},{11,1... | collective-permute-start | bytes 1179656 | tf_op jit(solution)/shard_map/ppermute | solution.py:190
  8.6 2.6 %collective-permute-start.1 = (bf16[256,768]{1,0:T(8,128)(2,1)}, bf16[256,768]{1,0:T(8,128)(2,1)S(1)}, u32[]{:S(2)}, u32[]{:S(2)}) collective-permute-start(bf16[256,768]{1,0:T(8,128)(2,1)} %x_ref.1), channel_id=1, source_target_pairs={{33,0},{34,1},{35,2},{32,3},{37,4},{38,5},{39,6},{36,7},{41,8},{42... | collective-permute-start | bytes 1179656 | tf_op jit(solution)/shard_map/ppermute | solution.py:190
  11.3 1.0 %collective-permute-start.4 = (bf16[256,768]{1,0:T(8,128)(2,1)}, bf16[256,768]{1,0:T(8,128)(2,1)S(1)}, u32[]{:S(2)}, u32[]{:S(2)}) collective-permute-start(bf16[256,768]{1,0:T(8,128)(2,1)} %x_ref.1), channel_id=1, source_target_pairs={{4,0},{5,1},{6,2},{7,3},{8,4},{9,5},{10,6},{11,7},{12,8},{13,9},{1... | collective-permute-start | bytes 1179656 | tf_op jit(solution)/shard_map/ppermute | solution.py:190
  12.3 0.0 copy-start.1
  12.3 0.7 %copy-done.1 = s32[256]{0:T(256)S(1)} copy-done((s32[256]{0:T(256)S(1)}, s32[256]{0:T(256)}, u32[]{:S(2)}) %copy-start.1) | copy-done | bytes 1048
  13.0 0.1 copy.3.column_ref
  13.1 0.1 stack.51.refs_0_
  13.2 0.0 copy-done
  13.2 0.2 shard_map.28.unit_ref.refs_1_
  13.4 0.3 shard_map.29.refs_7_
  13.7 0.1 collective-permute-done.x_ref
  13.8 2.5 %collective-permute-start.5 = (bf16[256,768]{1,0:T(8,128)(2,1)S(1)}, bf16[256,768]{1,0:T(8,128)(2,1)S(1)}, u32[]{:S(2)}, u32[]{:S(2)}) collective-permute-start(bf16[256,768]{1,0:T(8,128)(2,1)S(1)} %collective-permute-done.x_ref), channel_id=1, source_target_pairs={{4,0},{5,1},{6,2},{7,3},{8,4},{9,5},{10,6},{11,7},{12,8},{13,9},{1... | collective-permute-start | bytes 1179656 | tf_op jit(solution)/shard_map/ppermute | solution.py:190
  16.3 5.9 %collective-permute-done.2.x_ref = bf16[256,768]{1,0:T(8,128)(2,1)S(1)} collective-permute-done((bf16[256,768]{1,0:T(8,128)(2,1)}, bf16[256,768]{1,0:T(8,128)(2,1)S(1)}, u32[]{:S(2)}, u32[]{:S(2)}) %collective-permute-start.2) | collective-permute-done | bytes 393248 | tf_op jit(solution)/shard_map/ppermute | solution.py:190
  22.2 1.4 %collective-permute-start.7 = (bf16[256,768]{1,0:T(8,128)(2,1)S(1)}, bf16[256,768]{1,0:T(8,128)(2,1)S(1)}, u32[]{:S(2)}, u32[]{:S(2)}) collective-permute-start(bf16[256,768]{1,0:T(8,128)(2,1)S(1)} %collective-permute-done.2.x_ref), channel_id=1, source_target_pairs={{32,0},{33,1},{34,2},{35,3},{36,4},{37,5},{38,6},{39,7},{40,8},{41... | collective-permute-start | bytes 1179656 | tf_op jit(solution)/shard_map/ppermute | solution.py:190
  23.6 0.0 collective-permute-done.3.x_ref
  23.6 0.0 collective-permute-start.6
  23.6 0.0 collective-permute-done.1.x_ref
  23.6 2.0 %collective-permute-start.9 = (bf16[256,768]{1,0:T(8,128)(2,1)S(1)}, bf16[256,768]{1,0:T(8,128)(2,1)S(1)}, u32[]{:S(2)}, u32[]{:S(2)}) collective-permute-start(bf16[256,768]{1,0:T(8,128)(2,1)S(1)} %collective-permute-done.1.x_ref), channel_id=1, source_target_pairs={{3,0},{0,1},{1,2},{2,3},{7,4},{4,5},{5,6},{6,7},{11,8},{8,9},{9,10... | collective-permute-start | bytes 1179656 | tf_op jit(solution)/shard_map/ppermute | solution.py:190
  25.7 0.0 collective-permute-done.4.x_ref
  25.7 1.3 %collective-permute-start.8 = (bf16[256,768]{1,0:T(8,128)(2,1)S(1)}, bf16[256,768]{1,0:T(8,128)(2,1)S(1)}, u32[]{:S(2)}, u32[]{:S(2)}) collective-permute-start(bf16[256,768]{1,0:T(8,128)(2,1)S(1)} %collective-permute-done.1.x_ref), channel_id=1, source_target_pairs={{1,0},{2,1},{3,2},{0,3},{5,4},{6,5},{7,6},{4,7},{9,8},{10,9},{11,1... | collective-permute-start | bytes 1179656 | tf_op jit(solution)/shard_map/ppermute | solution.py:190
  27.0 0.0 collective-permute-done.5.x_ref
  27.0 0.1 collective-permute-start.10
  27.1 0.2 shard_map.30.refs_2_
  27.2 0.2 shard_map.31.refs_3_
  27.4 0.2 shard_map.32.refs_4_
  27.6 0.2 shard_map.33.refs_5_
  27.7 0.2 shard_map.34.refs_6_
  27.9 2.2 %shard_map.35.refs_10_ = f32[12,8,256]{2,1,0:T(8,128)S(1)} custom-call(s32[12]{0:T(128)S(1)} %stack.51.refs_0_, bf16[256,768]{1,0:T(8,128)(2,1)S(1)} %shard_map.28.unit_ref.refs_1_, bf16[256,768]{1,0:T(8,128)(2,1)S(1)} %shard_map.30.refs_2_, bf16[256,768]{1,0:T(8,128)(2,1)S(1)} %shard_map.31.refs_3_, bf16[256,768]{1,0:T(8,128)(2,1)S(1)} %shard_map.32.refs_4_, ...), custom_call_target="tpu_custom_call" | custom-call | flops 1308622848 | bytes 5111808 | tf_op jit(solution)/shard_map/pallas_call | solution.py:130
  30.1 1.4 %collective-permute-done.7.x_ref = bf16[256,768]{1,0:T(8,128)(2,1)S(1)} collective-permute-done((bf16[256,768]{1,0:T(8,128)(2,1)S(1)}, bf16[256,768]{1,0:T(8,128)(2,1)S(1)}, u32[]{:S(2)}, u32[]{:S(2)}) %collective-permute-start.7) | collective-permute-done | bytes 393248 | tf_op jit(solution)/shard_map/ppermute | solution.py:190
  31.5 1.5 %collective-permute-done.6.x_ref = bf16[256,768]{1,0:T(8,128)(2,1)S(1)} collective-permute-done((bf16[256,768]{1,0:T(8,128)(2,1)S(1)}, bf16[256,768]{1,0:T(8,128)(2,1)S(1)}, u32[]{:S(2)}, u32[]{:S(2)}) %collective-permute-start.6) | collective-permute-done | bytes 393248 | tf_op jit(solution)/shard_map/ppermute | solution.py:190
  33.0 0.2 shard_map.36.refs_7_
  33.2 0.2 shard_map.37.refs_8_
  33.4 0.2 shard_map.38.refs_9_
  33.5 1.8 %shard_map.39.refs_13_ = f32[12,8,256]{2,1,0:T(8,128)S(1)} custom-call(s32[12]{0:T(128)S(1)} %stack.51.refs_0_, bf16[256,768]{1,0:T(8,128)(2,1)S(1)} %shard_map.28.unit_ref.refs_1_, bf16[256,768]{1,0:T(8,128)(2,1)S(1)} %shard_map.30.refs_2_, bf16[256,768]{1,0:T(8,128)(2,1)S(1)} %shard_map.31.refs_3_, bf16[256,768]{1,0:T(8,128)(2,1)S(1)} %shard_map.32.refs_4_, ...), custom_call_target="tpu_custom_call" | custom-call | flops 1006632960 | bytes 3932160 | tf_op jit(solution)/shard_map/pallas_call | solution.py:130
  35.4 1.6 %collective-permute-done.9.x_ref = bf16[256,768]{1,0:T(8,128)(2,1)S(1)} collective-permute-done((bf16[256,768]{1,0:T(8,128)(2,1)S(1)}, bf16[256,768]{1,0:T(8,128)(2,1)S(1)}, u32[]{:S(2)}, u32[]{:S(2)}) %collective-permute-start.9) | collective-permute-done | bytes 393248 | tf_op jit(solution)/shard_map/ppermute | solution.py:190
  37.0 0.3 collective-permute-done.8.x_ref
  37.3 0.0 collective-permute-done.10.x_ref
  37.3 0.2 shard_map.40.refs_10_
  37.4 0.2 shard_map.41.refs_11_
  37.6 0.2 shard_map.42.refs_12_
  37.8 2.9 %shard_map.43 = (f32[8,1,256]{2,1,0:T(1,128)}, f32[1,256]{1,0:T(1,128)S(1)}, f32[1,256]{1,0:T(1,128)S(1)}, f32[1,256]{1,0:T(1,128)S(1)}) custom-call(s32[12]{0:T(128)S(1)} %stack.51.refs_0_, bf16[256,768]{1,0:T(8,128)(2,1)S(1)} %shard_map.28.unit_ref.refs_1_, bf16[256,768]{1,0:T(8,128)(2,1)S(1)} %shard_map.30.refs_2_, ...), custom_call_target="tpu_custom_call" | custom-call | flops 1409286144 | bytes 5505024 | tf_op jit(solution)/shard_map/pallas_call | solution.py:130
  40.7 7.9 %all-to-all-start = ((f32[8,1,256]{2,1,0:T(1,128)}), f32[8,1,256]{2,1,0:T(1,128)S(1)}, u32[]{:S(2)}, u32[]{:S(2)}) async-start(f32[8,1,256]{2,1,0:T(1,128)} %get-tuple-element.43), calls=%async_computation | async-start | bytes 16384 | tf_op jit(solution)/shard_map/all_to_all | solution.py:197
  48.6 0.0 collective-permute-start.11
  48.6 3.6 %collective-permute-start.12 = (f32[1,256]{1,0:T(1,128)S(1)}, f32[1,256]{1,0:T(1,128)S(1)}, u32[]{:S(2)}, u32[]{:S(2)}) collective-permute-start(f32[1,256]{1,0:T(1,128)S(1)} %get-tuple-element.45), channel_id=1, source_target_pairs={{0,8},{1,9},{2,10},{3,11},{4,12},{5,13},{6,14},{7,15},{8,16},{9,17... | collective-permute-start | bytes 3080 | tf_op jit(solution)/shard_map/ppermute | solution.py:194
  52.1 1.5 %collective-permute-start.13 = (f32[1,256]{1,0:T(1,128)S(1)}, f32[1,256]{1,0:T(1,128)S(1)}, u32[]{:S(2)}, u32[]{:S(2)}) collective-permute-start(f32[1,256]{1,0:T(1,128)S(1)} %get-tuple-element.46), channel_id=1, source_target_pairs={{0,12},{1,13},{2,14},{3,15},{4,16},{5,17},{6,18},{7,19},{8,20},{9,... | collective-permute-start | bytes 3080 | tf_op jit(solution)/shard_map/ppermute | solution.py:194
  53.6 0.0 collective-permute-done.11.refs_0_
  53.6 0.6 %collective-permute-done.12.refs_1_ = f32[1,256]{1,0:T(1,128)S(1)} collective-permute-done((f32[1,256]{1,0:T(1,128)S(1)}, f32[1,256]{1,0:T(1,128)S(1)}, u32[]{:S(2)}, u32[]{:S(2)}) %collective-permute-start.12) | collective-permute-done | bytes 1056 | tf_op jit(solution)/shard_map/ppermute | solution.py:194
  54.3 4.5 %collective-permute-done.13.refs_2_ = f32[1,256]{1,0:T(1,128)S(1)} collective-permute-done((f32[1,256]{1,0:T(1,128)S(1)}, f32[1,256]{1,0:T(1,128)S(1)}, u32[]{:S(2)}, u32[]{:S(2)}) %collective-permute-start.13) | collective-permute-done | bytes 1056 | tf_op jit(solution)/shard_map/ppermute | solution.py:194
  58.7 0.0 all-to-all-done.found_ref
  58.7 0.6 shard_map.44
Async XLA Ops:
  0.0 13.2 %copy-start = (bf16[256,768]{1,0:T(8,128)(2,1)S(1)}, bf16[256,768]{1,0:T(8,128)(2,1)}, u32[]{:S(2)}) copy-start(bf16[256,768]{1,0:T(8,128)(2,1)} %x_ref.1) | copy-start | bytes 1179652
  0.0 13.8 %collective-permute-start = (bf16[256,768]{1,0:T(8,128)(2,1)}, bf16[256,768]{1,0:T(8,128)(2,1)S(1)}, u32[]{:S(2)}, u32[]{:S(2)}) collective-permute-start(bf16[256,768]{1,0:T(8,128)(2,1)} %x_ref.1), channel_id=1, source_target_pairs={{8,0},{9,1},{10,2},{11,3},{12,4},{13,5},{14,6},{15,7},{16,8},{17,9... | collective-permute-start | bytes 1179656 | tf_op jit(solution)/shard_map/ppermute | solution.py:190
  5.4 16.8 %collective-permute-start.2 = (bf16[256,768]{1,0:T(8,128)(2,1)}, bf16[256,768]{1,0:T(8,128)(2,1)S(1)}, u32[]{:S(2)}, u32[]{:S(2)}) collective-permute-start(bf16[256,768]{1,0:T(8,128)(2,1)} %x_ref.1), channel_id=1, source_target_pairs={{3,0},{0,1},{1,2},{2,3},{7,4},{4,5},{5,6},{6,7},{11,8},{8,9},{9,10... | collective-permute-start | bytes 1179656 | tf_op jit(solution)/shard_map/ppermute | solution.py:190
  7.0 16.6 %collective-permute-start.3 = (bf16[256,768]{1,0:T(8,128)(2,1)}, bf16[256,768]{1,0:T(8,128)(2,1)S(1)}, u32[]{:S(2)}, u32[]{:S(2)}) collective-permute-start(bf16[256,768]{1,0:T(8,128)(2,1)} %x_ref.1), channel_id=1, source_target_pairs={{1,0},{2,1},{3,2},{0,3},{5,4},{6,5},{7,6},{4,7},{9,8},{10,9},{11,1... | collective-permute-start | bytes 1179656 | tf_op jit(solution)/shard_map/ppermute | solution.py:190
  8.6 15.0 %collective-permute-start.1 = (bf16[256,768]{1,0:T(8,128)(2,1)}, bf16[256,768]{1,0:T(8,128)(2,1)S(1)}, u32[]{:S(2)}, u32[]{:S(2)}) collective-permute-start(bf16[256,768]{1,0:T(8,128)(2,1)} %x_ref.1), channel_id=1, source_target_pairs={{33,0},{34,1},{35,2},{32,3},{37,4},{38,5},{39,6},{36,7},{41,8},{42... | collective-permute-start | bytes 1179656 | tf_op jit(solution)/shard_map/ppermute | solution.py:190
  11.3 14.4 %collective-permute-start.4 = (bf16[256,768]{1,0:T(8,128)(2,1)}, bf16[256,768]{1,0:T(8,128)(2,1)S(1)}, u32[]{:S(2)}, u32[]{:S(2)}) collective-permute-start(bf16[256,768]{1,0:T(8,128)(2,1)} %x_ref.1), channel_id=1, source_target_pairs={{4,0},{5,1},{6,2},{7,3},{8,4},{9,5},{10,6},{11,7},{12,8},{13,9},{1... | collective-permute-start | bytes 1179656 | tf_op jit(solution)/shard_map/ppermute | solution.py:190
  12.3 0.7 %copy-start.1 = (s32[256]{0:T(256)S(1)}, s32[256]{0:T(256)}, u32[]{:S(2)}) copy-start(s32[256]{0:T(256)} %param.3) | copy-start | bytes 3076
  13.8 13.1 %collective-permute-start.5 = (bf16[256,768]{1,0:T(8,128)(2,1)S(1)}, bf16[256,768]{1,0:T(8,128)(2,1)S(1)}, u32[]{:S(2)}, u32[]{:S(2)}) collective-permute-start(bf16[256,768]{1,0:T(8,128)(2,1)S(1)} %collective-permute-done.x_ref), channel_id=1, source_target_pairs={{4,0},{5,1},{6,2},{7,3},{8,4},{9,5},{10,6},{11,7},{12,8},{13,9},{1... | collective-permute-start | bytes 1179656 | tf_op jit(solution)/shard_map/ppermute | solution.py:190
  22.2 9.3 %collective-permute-start.7 = (bf16[256,768]{1,0:T(8,128)(2,1)S(1)}, bf16[256,768]{1,0:T(8,128)(2,1)S(1)}, u32[]{:S(2)}, u32[]{:S(2)}) collective-permute-start(bf16[256,768]{1,0:T(8,128)(2,1)S(1)} %collective-permute-done.2.x_ref), channel_id=1, source_target_pairs={{32,0},{33,1},{34,2},{35,3},{36,4},{37,5},{38,6},{39,7},{40,8},{41... | collective-permute-start | bytes 1179656 | tf_op jit(solution)/shard_map/ppermute | solution.py:190
  23.6 9.4 %collective-permute-start.6 = (bf16[256,768]{1,0:T(8,128)(2,1)S(1)}, bf16[256,768]{1,0:T(8,128)(2,1)S(1)}, u32[]{:S(2)}, u32[]{:S(2)}) collective-permute-start(bf16[256,768]{1,0:T(8,128)(2,1)S(1)} %collective-permute-done.3.x_ref), channel_id=1, source_target_pairs={{1,0},{2,1},{3,2},{0,3},{5,4},{6,5},{7,6},{4,7},{9,8},{10,9},{11,1... | collective-permute-start | bytes 1179656 | tf_op jit(solution)/shard_map/ppermute | solution.py:190
  23.6 13.3 %collective-permute-start.9 = (bf16[256,768]{1,0:T(8,128)(2,1)S(1)}, bf16[256,768]{1,0:T(8,128)(2,1)S(1)}, u32[]{:S(2)}, u32[]{:S(2)}) collective-permute-start(bf16[256,768]{1,0:T(8,128)(2,1)S(1)} %collective-permute-done.1.x_ref), channel_id=1, source_target_pairs={{3,0},{0,1},{1,2},{2,3},{7,4},{4,5},{5,6},{6,7},{11,8},{8,9},{9,10... | collective-permute-start | bytes 1179656 | tf_op jit(solution)/shard_map/ppermute | solution.py:190
  25.7 11.6 %collective-permute-start.8 = (bf16[256,768]{1,0:T(8,128)(2,1)S(1)}, bf16[256,768]{1,0:T(8,128)(2,1)S(1)}, u32[]{:S(2)}, u32[]{:S(2)}) collective-permute-start(bf16[256,768]{1,0:T(8,128)(2,1)S(1)} %collective-permute-done.1.x_ref), channel_id=1, source_target_pairs={{1,0},{2,1},{3,2},{0,3},{5,4},{6,5},{7,6},{4,7},{9,8},{10,9},{11,1... | collective-permute-start | bytes 1179656 | tf_op jit(solution)/shard_map/ppermute | solution.py:190
  27.0 10.3 %collective-permute-start.10 = (bf16[256,768]{1,0:T(8,128)(2,1)S(1)}, bf16[256,768]{1,0:T(8,128)(2,1)S(1)}, u32[]{:S(2)}, u32[]{:S(2)}) collective-permute-start(bf16[256,768]{1,0:T(8,128)(2,1)S(1)} %collective-permute-done.5.x_ref), channel_id=1, source_target_pairs={{4,0},{5,1},{6,2},{7,3},{8,4},{9,5},{10,6},{11,7},{12,8},{13,9},{1... | collective-permute-start | bytes 1179656 | tf_op jit(solution)/shard_map/ppermute | solution.py:190
  40.7 18.1 %all-to-all-start = ((f32[8,1,256]{2,1,0:T(1,128)}), f32[8,1,256]{2,1,0:T(1,128)S(1)}, u32[]{:S(2)}, u32[]{:S(2)}) async-start(f32[8,1,256]{2,1,0:T(1,128)} %get-tuple-element.43), calls=%async_computation | async-start | bytes 16384 | tf_op jit(solution)/shard_map/all_to_all | solution.py:197
  48.6 5.1 %collective-permute-start.11 = (f32[1,256]{1,0:T(1,128)S(1)}, f32[1,256]{1,0:T(1,128)S(1)}, u32[]{:S(2)}, u32[]{:S(2)}) collective-permute-start(f32[1,256]{1,0:T(1,128)S(1)} %get-tuple-element.44), channel_id=1, source_target_pairs={{0,4},{1,5},{2,6},{3,7},{4,8},{5,9},{6,10},{7,11},{8,12},{9,13},{1... | collective-permute-start | bytes 3080 | tf_op jit(solution)/shard_map/ppermute | solution.py:194
  48.6 5.7 %collective-permute-start.12 = (f32[1,256]{1,0:T(1,128)S(1)}, f32[1,256]{1,0:T(1,128)S(1)}, u32[]{:S(2)}, u32[]{:S(2)}) collective-permute-start(f32[1,256]{1,0:T(1,128)S(1)} %get-tuple-element.45), channel_id=1, source_target_pairs={{0,8},{1,9},{2,10},{3,11},{4,12},{5,13},{6,14},{7,15},{8,16},{9,17... | collective-permute-start | bytes 3080 | tf_op jit(solution)/shard_map/ppermute | solution.py:194
  52.1 6.6 %collective-permute-start.13 = (f32[1,256]{1,0:T(1,128)S(1)}, f32[1,256]{1,0:T(1,128)S(1)}, u32[]{:S(2)}, u32[]{:S(2)}) collective-permute-start(f32[1,256]{1,0:T(1,128)S(1)} %get-tuple-element.46), channel_id=1, source_target_pairs={{0,12},{1,13},{2,14},{3,15},{4,16},{5,17},{6,18},{7,19},{8,20},{9,... | collective-permute-start | bytes 3080 | tf_op jit(solution)/shard_map/ppermute | solution.py:194
where the time goes:
time: 59.4 us; the launch traced here: 59.3 us
  starting transfers between devices  32.6 us (55%)
  waiting for transfers between devices  16 us (27%)
  Pallas kernels  9.74 us (16%)
  local copies, waits for them, and re-layouts  0.91 us (2%)
    ppermute x11, starting transfers between devices, per_device(): lax.ppermute(blocks[slot], BOTH, shift_pairs(shift, False, clusters, memb...  19.6 us
    ppermute x11, waiting for transfers between devices, per_device(): lax.ppermute(blocks[slot], BOTH, shift_pairs(shift, False, clusters, memb...  10.9 us
    all_to_all x1, starting transfers between devices, per_device(): lax.all_to_all(best, 'members', 0, 0, axis_index_groups=plane_groups(memb...  7.93 us
    pallas_call x5, Pallas kernels, call_kernel(): pl.pallas_call(kernel, out_shape=[jax.ShapeDtypeStruct(one, jnp.float32)...  7.79 us
    ppermute x3, waiting for transfers between devices, per_device(): lax.ppermute(row, BOTH, shift_pairs(places[slot], True, clusters, members))  5.08 us
    ppermute x3, starting transfers between devices, per_device(): lax.ppermute(row, BOTH, shift_pairs(places[slot], True, clusters, members))  5.05 us
    pallas_call x12, Pallas kernels, normalize(): pl.pallas_call(normalize_kernel, out_shape=jax.ShapeDtypeStruct(embedding...  1.95 us
  transfers between devices with their start and end apart: 15, of which 8 were waited for; matrix products, arithmetic and copies ran while one was open for 0% of the time, Pallas kernels for 10%

commit v1 on v0

--- a/solution.py
+++ b/solution.py
@@ -7,7 +7,7 @@
 
 SIZES = (2, 8, 4)
 SENDS = [((0,), (0, 2, 0)), ((0,), (1, 0, 1)), ((0,), (0, 0, -1)), ((0,), (0, 0, 1)), ((0,), (0, 1, 0)), ((1,), (0, 1, 0)), ((4,), (0, 0, 1)), ((3,), (1, 0, 0)), ((2,), (0, 0, 1)), ((2,), (0, 0, -1)), ((6,), (0, 1, 0))]
-ROWS = [5, 1, 6]
+ROWS = [6, 1, 5]
 STAGES = [[(1, 0), (2, 0), (2, 1), (3, 0), (3, 1), (3, 2), (4, 1), (4, 2), (4, 3), (5, 0), (5, 2), (5, 3), (5, 4)], [(6, 0), (6, 2), (6, 3), (6, 4), (7, 1), (7, 5), (7, 6), (8, 1), (8, 5), (8, 6)], [(11, 0), (11, 2), (11, 3), (11, 4), (11, 7), (11, 8), (11, 9), (11, 10), (9, 1), (9, 5), (9, 6), (10, 1), (10, 5), (10, 6)]]
 FIRST = 6
 HELD = (1,)

time: 59.4 us -> 59.1 us (level)
  the two profiles are of different devices: /device:TPU:38 before, /device:TPU:6 now
where the time goes in v1:
time: 59.1 us; the launch traced here: 59 us
  starting transfers between devices  37.2 us (63%)
  waiting for transfers between devices  11 us (19%)
  Pallas kernels  9.75 us (16%)
  local copies, waits for them, and re-layouts  0.91 us (2%)
    ppermute x11, starting transfers between devices, per_device(): lax.ppermute(blocks[slot], BOTH, shift_pairs(shift, False, clusters, memb...  23.1 us
    pallas_call x5, Pallas kernels, call_kernel(): pl.pallas_call(kernel, out_shape=[jax.ShapeDtypeStruct(one, jnp.float32)...  7.8 us
    all_to_all x1, starting transfers between devices, per_device(): lax.all_to_all(best, 'members', 0, 0, axis_index_groups=plane_groups(memb...  7.22 us
    ppermute x11, waiting for transfers between devices, per_device(): lax.ppermute(blocks[slot], BOTH, shift_pairs(shift, False, clusters, memb...  7.11 us
    ppermute x3, starting transfers between devices, per_device(): lax.ppermute(row, BOTH, shift_pairs(places[slot], True, clusters, members))  6.95 us
    ppermute x3, waiting for transfers between devices, per_device(): lax.ppermute(row, BOTH, shift_pairs(places[slot], True, clusters, members))  3.88 us
    pallas_call x12, Pallas kernels, normalize(): pl.pallas_call(normalize_kernel, out_shape=jax.ShapeDtypeStruct(embedding...  1.95 us
  transfers between devices with their start and end apart: 15, of which 5 were waited for; matrix products, arithmetic and copies ran while one was open for 0% of the time, Pallas kernels for 10%

profile of v1, /device:TPU:6, one launch (start us, length us, event | category | flops | bytes accessed | tf_op | source)
XLA Modules:
  0.0 59.0 jit_solution(15060536690821592822)
XLA Ops:
  0.0 0.0 copy-start
  0.0 6.3 %collective-permute-start = (bf16[256,768]{1,0:T(8,128)(2,1)}, bf16[256,768]{1,0:T(8,128)(2,1)S(1)}, u32[]{:S(2)}, u32[]{:S(2)}) collective-permute-start(bf16[256,768]{1,0:T(8,128)(2,1)} %x_ref.1), channel_id=1, source_target_pairs={{8,0},{9,1},{10,2},{11,3},{12,4},{13,5},{14,6},{15,7},{16,8},{17,9... | collective-permute-start | bytes 1179656 | tf_op jit(solution)/shard_map/ppermute | solution.py:190
  6.3 1.6 %collective-permute-start.2 = (bf16[256,768]{1,0:T(8,128)(2,1)}, bf16[256,768]{1,0:T(8,128)(2,1)S(1)}, u32[]{:S(2)}, u32[]{:S(2)}) collective-permute-start(bf16[256,768]{1,0:T(8,128)(2,1)} %x_ref.1), channel_id=1, source_target_pairs={{3,0},{0,1},{1,2},{2,3},{7,4},{4,5},{5,6},{6,7},{11,8},{8,9},{9,10... | collective-permute-start | bytes 1179656 | tf_op jit(solution)/shard_map/ppermute | solution.py:190
  7.9 1.7 %collective-permute-start.3 = (bf16[256,768]{1,0:T(8,128)(2,1)}, bf16[256,768]{1,0:T(8,128)(2,1)S(1)}, u32[]{:S(2)}, u32[]{:S(2)}) collective-permute-start(bf16[256,768]{1,0:T(8,128)(2,1)} %x_ref.1), channel_id=1, source_target_pairs={{1,0},{2,1},{3,2},{0,3},{5,4},{6,5},{7,6},{4,7},{9,8},{10,9},{11,1... | collective-permute-start | bytes 1179656 | tf_op jit(solution)/shard_map/ppermute | solution.py:190
  9.5 2.6 %collective-permute-start.1 = (bf16[256,768]{1,0:T(8,128)(2,1)}, bf16[256,768]{1,0:T(8,128)(2,1)S(1)}, u32[]{:S(2)}, u32[]{:S(2)}) collective-permute-start(bf16[256,768]{1,0:T(8,128)(2,1)} %x_ref.1), channel_id=1, source_target_pairs={{33,0},{34,1},{35,2},{32,3},{37,4},{38,5},{39,6},{36,7},{41,8},{42... | collective-permute-start | bytes 1179656 | tf_op jit(solution)/shard_map/ppermute | solution.py:190
  12.2 1.0 %collective-permute-start.4 = (bf16[256,768]{1,0:T(8,128)(2,1)}, bf16[256,768]{1,0:T(8,128)(2,1)S(1)}, u32[]{:S(2)}, u32[]{:S(2)}) collective-permute-start(bf16[256,768]{1,0:T(8,128)(2,1)} %x_ref.1), channel_id=1, source_target_pairs={{4,0},{5,1},{6,2},{7,3},{8,4},{9,5},{10,6},{11,7},{12,8},{13,9},{1... | collective-permute-start | bytes 1179656 | tf_op jit(solution)/shard_map/ppermute | solution.py:190
  13.2 0.0 copy-start.1
  13.2 0.7 %copy-done.1 = s32[256]{0:T(256)S(1)} copy-done((s32[256]{0:T(256)S(1)}, s32[256]{0:T(256)}, u32[]{:S(2)}) %copy-start.1) | copy-done | bytes 1048
  13.9 0.1 copy.3.column_ref
  14.0 0.1 stack.51.refs_0_
  14.1 0.0 copy-done
  14.1 0.2 shard_map.28.unit_ref.refs_1_
  14.3 0.3 shard_map.29.refs_7_
  14.6 1.6 %collective-permute-done.x_ref = bf16[256,768]{1,0:T(8,128)(2,1)S(1)} collective-permute-done((bf16[256,768]{1,0:T(8,128)(2,1)}, bf16[256,768]{1,0:T(8,128)(2,1)S(1)}, u32[]{:S(2)}, u32[]{:S(2)}) %collective-permute-start) | collective-permute-done | bytes 393248 | tf_op jit(solution)/shard_map/ppermute | solution.py:190
  16.2 2.7 %collective-permute-start.5 = (bf16[256,768]{1,0:T(8,128)(2,1)S(1)}, bf16[256,768]{1,0:T(8,128)(2,1)S(1)}, u32[]{:S(2)}, u32[]{:S(2)}) collective-permute-start(bf16[256,768]{1,0:T(8,128)(2,1)S(1)} %collective-permute-done.x_ref), channel_id=1, source_target_pairs={{4,0},{5,1},{6,2},{7,3},{8,4},{9,5},{10,6},{11,7},{12,8},{13,9},{1... | collective-permute-start | bytes 1179656 | tf_op jit(solution)/shard_map/ppermute | solution.py:190
  18.8 3.4 %collective-permute-done.2.x_ref = bf16[256,768]{1,0:T(8,128)(2,1)S(1)} collective-permute-done((bf16[256,768]{1,0:T(8,128)(2,1)}, bf16[256,768]{1,0:T(8,128)(2,1)S(1)}, u32[]{:S(2)}, u32[]{:S(2)}) %collective-permute-start.2) | collective-permute-done | bytes 393248 | tf_op jit(solution)/shard_map/ppermute | solution.py:190
  22.2 1.4 %collective-permute-start.7 = (bf16[256,768]{1,0:T(8,128)(2,1)S(1)}, bf16[256,768]{1,0:T(8,128)(2,1)S(1)}, u32[]{:S(2)}, u32[]{:S(2)}) collective-permute-start(bf16[256,768]{1,0:T(8,128)(2,1)S(1)} %collective-permute-done.2.x_ref), channel_id=1, source_target_pairs={{32,0},{33,1},{34,2},{35,3},{36,4},{37,5},{38,6},{39,7},{40,8},{41... | collective-permute-start | bytes 1179656 | tf_op jit(solution)/shard_map/ppermute | solution.py:190
  23.6 0.0 collective-permute-done.3.x_ref
  23.6 0.0 collective-permute-start.6
  23.6 0.0 collective-permute-done.1.x_ref
  23.6 2.0 %collective-permute-start.9 = (bf16[256,768]{1,0:T(8,128)(2,1)S(1)}, bf16[256,768]{1,0:T(8,128)(2,1)S(1)}, u32[]{:S(2)}, u32[]{:S(2)}) collective-permute-start(bf16[256,768]{1,0:T(8,128)(2,1)S(1)} %collective-permute-done.1.x_ref), channel_id=1, source_target_pairs={{3,0},{0,1},{1,2},{2,3},{7,4},{4,5},{5,6},{6,7},{11,8},{8,9},{9,10... | collective-permute-start | bytes 1179656 | tf_op jit(solution)/shard_map/ppermute | solution.py:190
  25.7 0.0 collective-permute-done.4.x_ref
  25.7 1.3 %collective-permute-start.8 = (bf16[256,768]{1,0:T(8,128)(2,1)S(1)}, bf16[256,768]{1,0:T(8,128)(2,1)S(1)}, u32[]{:S(2)}, u32[]{:S(2)}) collective-permute-start(bf16[256,768]{1,0:T(8,128)(2,1)S(1)} %collective-permute-done.1.x_ref), channel_id=1, source_target_pairs={{1,0},{2,1},{3,2},{0,3},{5,4},{6,5},{7,6},{4,7},{9,8},{10,9},{11,1... | collective-permute-start | bytes 1179656 | tf_op jit(solution)/shard_map/ppermute | solution.py:190
  27.0 0.0 collective-permute-done.5.x_ref
  27.0 2.5 %collective-permute-start.10 = (bf16[256,768]{1,0:T(8,128)(2,1)S(1)}, bf16[256,768]{1,0:T(8,128)(2,1)S(1)}, u32[]{:S(2)}, u32[]{:S(2)}) collective-permute-start(bf16[256,768]{1,0:T(8,128)(2,1)S(1)} %collective-permute-done.5.x_ref), channel_id=1, source_target_pairs={{4,0},{5,1},{6,2},{7,3},{8,4},{9,5},{10,6},{11,7},{12,8},{13,9},{1... | collective-permute-start | bytes 1179656 | tf_op jit(solution)/shard_map/ppermute | solution.py:190
  29.5 0.2 shard_map.30.refs_2_
  29.6 0.2 shard_map.31.refs_3_
  29.8 0.2 shard_map.32.refs_4_
  29.9 0.2 shard_map.33.refs_5_
  30.1 0.2 shard_map.34.refs_6_
  30.3 2.2 %shard_map.35.refs_10_ = f32[12,8,256]{2,1,0:T(8,128)S(1)} custom-call(s32[12]{0:T(128)S(1)} %stack.51.refs_0_, bf16[256,768]{1,0:T(8,128)(2,1)S(1)} %shard_map.28.unit_ref.refs_1_, bf16[256,768]{1,0:T(8,128)(2,1)S(1)} %shard_map.30.refs_2_, bf16[256,768]{1,0:T(8,128)(2,1)S(1)} %shard_map.31.refs_3_, bf16[256,768]{1,0:T(8,128)(2,1)S(1)} %shard_map.32.refs_4_, ...), custom_call_target="tpu_custom_call" | custom-call | flops 1308622848 | bytes 5111808 | tf_op jit(solution)/shard_map/pallas_call | solution.py:130
  32.5 0.0 collective-permute-done.7.x_ref
  32.5 0.0 collective-permute-done.6.x_ref
  32.5 0.2 shard_map.36.refs_7_
  32.7 0.2 shard_map.37.refs_8_
  32.8 0.2 shard_map.38.refs_9_
  33.0 1.9 %shard_map.39.refs_13_ = f32[12,8,256]{2,1,0:T(8,128)S(1)} custom-call(s32[12]{0:T(128)S(1)} %stack.51.refs_0_, bf16[256,768]{1,0:T(8,128)(2,1)S(1)} %shard_map.28.unit_ref.refs_1_, bf16[256,768]{1,0:T(8,128)(2,1)S(1)} %shard_map.30.refs_2_, bf16[256,768]{1,0:T(8,128)(2,1)S(1)} %shard_map.31.refs_3_, bf16[256,768]{1,0:T(8,128)(2,1)S(1)} %shard_map.32.refs_4_, ...), custom_call_target="tpu_custom_call" | custom-call | flops 1006632960 | bytes 3932160 | tf_op jit(solution)/shard_map/pallas_call | solution.py:130
  34.8 2.1 %collective-permute-done.9.x_ref = bf16[256,768]{1,0:T(8,128)(2,1)S(1)} collective-permute-done((bf16[256,768]{1,0:T(8,128)(2,1)S(1)}, bf16[256,768]{1,0:T(8,128)(2,1)S(1)}, u32[]{:S(2)}, u32[]{:S(2)}) %collective-permute-start.9) | collective-permute-done | bytes 393248 | tf_op jit(solution)/shard_map/ppermute | solution.py:190
  37.0 0.0 collective-permute-done.8.x_ref
  37.0 0.0 collective-permute-done.10.x_ref
  37.0 0.2 shard_map.40.refs_10_
  37.2 0.2 shard_map.41.refs_11_
  37.3 0.2 shard_map.42.refs_12_
  37.5 2.9 %shard_map.43 = (f32[8,1,256]{2,1,0:T(1,128)}, f32[1,256]{1,0:T(1,128)S(1)}, f32[1,256]{1,0:T(1,128)S(1)}, f32[1,256]{1,0:T(1,128)S(1)}) custom-call(s32[12]{0:T(128)S(1)} %stack.51.refs_0_, bf16[256,768]{1,0:T(8,128)(2,1)S(1)} %shard_map.28.unit_ref.refs_1_, bf16[256,768]{1,0:T(8,128)(2,1)S(1)} %shard_map.30.refs_2_, ...), custom_call_target="tpu_custom_call" | custom-call | flops 1409286144 | bytes 5505024 | tf_op jit(solution)/shard_map/pallas_call | solution.py:130
  40.4 7.2 %all-to-all-start = ((f32[8,1,256]{2,1,0:T(1,128)}), f32[8,1,256]{2,1,0:T(1,128)S(1)}, u32[]{:S(2)}, u32[]{:S(2)}) async-start(f32[8,1,256]{2,1,0:T(1,128)} %get-tuple-element.43), calls=%async_computation | async-start | bytes 16384 | tf_op jit(solution)/shard_map/all_to_all | solution.py:197
  47.6 1.5 %collective-permute-start.11 = (f32[1,256]{1,0:T(1,128)S(1)}, f32[1,256]{1,0:T(1,128)S(1)}, u32[]{:S(2)}, u32[]{:S(2)}) collective-permute-start(f32[1,256]{1,0:T(1,128)S(1)} %get-tuple-element.44), channel_id=1, source_target_pairs={{0,12},{1,13},{2,14},{3,15},{4,16},{5,17},{6,18},{7,19},{8,20},{9,... | collective-permute-start | bytes 3080 | tf_op jit(solution)/shard_map/ppermute | solution.py:194
  49.0 4.6 %collective-permute-start.12 = (f32[1,256]{1,0:T(1,128)S(1)}, f32[1,256]{1,0:T(1,128)S(1)}, u32[]{:S(2)}, u32[]{:S(2)}) collective-permute-start(f32[1,256]{1,0:T(1,128)S(1)} %get-tuple-element.45), channel_id=1, source_target_pairs={{0,8},{1,9},{2,10},{3,11},{4,12},{5,13},{6,14},{7,15},{8,16},{9,17... | collective-permute-start | bytes 3080 | tf_op jit(solution)/shard_map/ppermute | solution.py:194
  53.6 0.9 %collective-permute-start.13 = (f32[1,256]{1,0:T(1,128)S(1)}, f32[1,256]{1,0:T(1,128)S(1)}, u32[]{:S(2)}, u32[]{:S(2)}) collective-permute-start(f32[1,256]{1,0:T(1,128)S(1)} %get-tuple-element.46), channel_id=1, source_target_pairs={{0,4},{1,5},{2,6},{3,7},{4,8},{5,9},{6,10},{7,11},{8,12},{9,13},{1... | collective-permute-start | bytes 3080 | tf_op jit(solution)/shard_map/ppermute | solution.py:194
  54.5 0.0 collective-permute-done.11.refs_0_
  54.5 1.1 %collective-permute-done.12.refs_1_ = f32[1,256]{1,0:T(1,128)S(1)} collective-permute-done((f32[1,256]{1,0:T(1,128)S(1)}, f32[1,256]{1,0:T(1,128)S(1)}, u32[]{:S(2)}, u32[]{:S(2)}) %collective-permute-start.12) | collective-permute-done | bytes 1056 | tf_op jit(solution)/shard_map/ppermute | solution.py:194
  55.6 2.8 %collective-permute-done.13.refs_2_ = f32[1,256]{1,0:T(1,128)S(1)} collective-permute-done((f32[1,256]{1,0:T(1,128)S(1)}, f32[1,256]{1,0:T(1,128)S(1)}, u32[]{:S(2)}, u32[]{:S(2)}) %collective-permute-start.13) | collective-permute-done | bytes 1056 | tf_op jit(solution)/shard_map/ppermute | solution.py:194
  58.4 0.0 all-to-all-done.found_ref
  58.4 0.6 shard_map.44
Async XLA Ops:
  0.0 14.1 %copy-start = (bf16[256,768]{1,0:T(8,128)(2,1)S(1)}, bf16[256,768]{1,0:T(8,128)(2,1)}, u32[]{:S(2)}) copy-start(bf16[256,768]{1,0:T(8,128)(2,1)} %x_ref.1) | copy-start | bytes 1179652
  0.0 16.2 %collective-permute-start = (bf16[256,768]{1,0:T(8,128)(2,1)}, bf16[256,768]{1,0:T(8,128)(2,1)S(1)}, u32[]{:S(2)}, u32[]{:S(2)}) collective-permute-start(bf16[256,768]{1,0:T(8,128)(2,1)} %x_ref.1), channel_id=1, source_target_pairs={{8,0},{9,1},{10,2},{11,3},{12,4},{13,5},{14,6},{15,7},{16,8},{17,9... | collective-permute-start | bytes 1179656 | tf_op jit(solution)/shard_map/ppermute | solution.py:190
  6.3 15.9 %collective-permute-start.2 = (bf16[256,768]{1,0:T(8,128)(2,1)}, bf16[256,768]{1,0:T(8,128)(2,1)S(1)}, u32[]{:S(2)}, u32[]{:S(2)}) collective-permute-start(bf16[256,768]{1,0:T(8,128)(2,1)} %x_ref.1), channel_id=1, source_target_pairs={{3,0},{0,1},{1,2},{2,3},{7,4},{4,5},{5,6},{6,7},{11,8},{8,9},{9,10... | collective-permute-start | bytes 1179656 | tf_op jit(solution)/shard_map/ppermute | solution.py:190
  7.9 15.7 %collective-permute-start.3 = (bf16[256,768]{1,0:T(8,128)(2,1)}, bf16[256,768]{1,0:T(8,128)(2,1)S(1)}, u32[]{:S(2)}, u32[]{:S(2)}) collective-permute-start(bf16[256,768]{1,0:T(8,128)(2,1)} %x_ref.1), channel_id=1, source_target_pairs={{1,0},{2,1},{3,2},{0,3},{5,4},{6,5},{7,6},{4,7},{9,8},{10,9},{11,1... | collective-permute-start | bytes 1179656 | tf_op jit(solution)/shard_map/ppermute | solution.py:190
  9.5 14.1 %collective-permute-start.1 = (bf16[256,768]{1,0:T(8,128)(2,1)}, bf16[256,768]{1,0:T(8,128)(2,1)S(1)}, u32[]{:S(2)}, u32[]{:S(2)}) collective-permute-start(bf16[256,768]{1,0:T(8,128)(2,1)} %x_ref.1), channel_id=1, source_target_pairs={{33,0},{34,1},{35,2},{32,3},{37,4},{38,5},{39,6},{36,7},{41,8},{42... | collective-permute-start | bytes 1179656 | tf_op jit(solution)/shard_map/ppermute | solution.py:190
  12.2 13.5 %collective-permute-start.4 = (bf16[256,768]{1,0:T(8,128)(2,1)}, bf16[256,768]{1,0:T(8,128)(2,1)S(1)}, u32[]{:S(2)}, u32[]{:S(2)}) collective-permute-start(bf16[256,768]{1,0:T(8,128)(2,1)} %x_ref.1), channel_id=1, source_target_pairs={{4,0},{5,1},{6,2},{7,3},{8,4},{9,5},{10,6},{11,7},{12,8},{13,9},{1... | collective-permute-start | bytes 1179656 | tf_op jit(solution)/shard_map/ppermute | solution.py:190
  13.2 0.7 %copy-start.1 = (s32[256]{0:T(256)S(1)}, s32[256]{0:T(256)}, u32[]{:S(2)}) copy-start(s32[256]{0:T(256)} %param.3) | copy-start | bytes 3076
  16.2 10.8 %collective-permute-start.5 = (bf16[256,768]{1,0:T(8,128)(2,1)S(1)}, bf16[256,768]{1,0:T(8,128)(2,1)S(1)}, u32[]{:S(2)}, u32[]{:S(2)}) collective-permute-start(bf16[256,768]{1,0:T(8,128)(2,1)S(1)} %collective-permute-done.x_ref), channel_id=1, source_target_pairs={{4,0},{5,1},{6,2},{7,3},{8,4},{9,5},{10,6},{11,7},{12,8},{13,9},{1... | collective-permute-start | bytes 1179656 | tf_op jit(solution)/shard_map/ppermute | solution.py:190
  22.2 10.3 %collective-permute-start.7 = (bf16[256,768]{1,0:T(8,128)(2,1)S(1)}, bf16[256,768]{1,0:T(8,128)(2,1)S(1)}, u32[]{:S(2)}, u32[]{:S(2)}) collective-permute-start(bf16[256,768]{1,0:T(8,128)(2,1)S(1)} %collective-permute-done.2.x_ref), channel_id=1, source_target_pairs={{32,0},{33,1},{34,2},{35,3},{36,4},{37,5},{38,6},{39,7},{40,8},{41... | collective-permute-start | bytes 1179656 | tf_op jit(solution)/shard_map/ppermute | solution.py:190
  23.6 8.9 %collective-permute-start.6 = (bf16[256,768]{1,0:T(8,128)(2,1)S(1)}, bf16[256,768]{1,0:T(8,128)(2,1)S(1)}, u32[]{:S(2)}, u32[]{:S(2)}) collective-permute-start(bf16[256,768]{1,0:T(8,128)(2,1)S(1)} %collective-permute-done.3.x_ref), channel_id=1, source_target_pairs={{1,0},{2,1},{3,2},{0,3},{5,4},{6,5},{7,6},{4,7},{9,8},{10,9},{11,1... | collective-permute-start | bytes 1179656 | tf_op jit(solution)/shard_map/ppermute | solution.py:190
  23.6 13.3 %collective-permute-start.9 = (bf16[256,768]{1,0:T(8,128)(2,1)S(1)}, bf16[256,768]{1,0:T(8,128)(2,1)S(1)}, u32[]{:S(2)}, u32[]{:S(2)}) collective-permute-start(bf16[256,768]{1,0:T(8,128)(2,1)S(1)} %collective-permute-done.1.x_ref), channel_id=1, source_target_pairs={{3,0},{0,1},{1,2},{2,3},{7,4},{4,5},{5,6},{6,7},{11,8},{8,9},{9,10... | collective-permute-start | bytes 1179656 | tf_op jit(solution)/shard_map/ppermute | solution.py:190
  25.7 11.3 %collective-permute-start.8 = (bf16[256,768]{1,0:T(8,128)(2,1)S(1)}, bf16[256,768]{1,0:T(8,128)(2,1)S(1)}, u32[]{:S(2)}, u32[]{:S(2)}) collective-permute-start(bf16[256,768]{1,0:T(8,128)(2,1)S(1)} %collective-permute-done.1.x_ref), channel_id=1, source_target_pairs={{1,0},{2,1},{3,2},{0,3},{5,4},{6,5},{7,6},{4,7},{9,8},{10,9},{11,1... | collective-permute-start | bytes 1179656 | tf_op jit(solution)/shard_map/ppermute | solution.py:190
  27.0 10.0 %collective-permute-start.10 = (bf16[256,768]{1,0:T(8,128)(2,1)S(1)}, bf16[256,768]{1,0:T(8,128)(2,1)S(1)}, u32[]{:S(2)}, u32[]{:S(2)}) collective-permute-start(bf16[256,768]{1,0:T(8,128)(2,1)S(1)} %collective-permute-done.5.x_ref), channel_id=1, source_target_pairs={{4,0},{5,1},{6,2},{7,3},{8,4},{9,5},{10,6},{11,7},{12,8},{13,9},{1... | collective-permute-start | bytes 1179656 | tf_op jit(solution)/shard_map/ppermute | solution.py:190
  40.4 18.0 %all-to-all-start = ((f32[8,1,256]{2,1,0:T(1,128)}), f32[8,1,256]{2,1,0:T(1,128)S(1)}, u32[]{:S(2)}, u32[]{:S(2)}) async-start(f32[8,1,256]{2,1,0:T(1,128)} %get-tuple-element.43), calls=%async_computation | async-start | bytes 16384 | tf_op jit(solution)/shard_map/all_to_all | solution.py:197
  47.6 6.9 %collective-permute-start.11 = (f32[1,256]{1,0:T(1,128)S(1)}, f32[1,256]{1,0:T(1,128)S(1)}, u32[]{:S(2)}, u32[]{:S(2)}) collective-permute-start(f32[1,256]{1,0:T(1,128)S(1)} %get-tuple-element.44), channel_id=1, source_target_pairs={{0,12},{1,13},{2,14},{3,15},{4,16},{5,17},{6,18},{7,19},{8,20},{9,... | collective-permute-start | bytes 3080 | tf_op jit(solution)/shard_map/ppermute | solution.py:194
  49.0 6.6 %collective-permute-start.12 = (f32[1,256]{1,0:T(1,128)S(1)}, f32[1,256]{1,0:T(1,128)S(1)}, u32[]{:S(2)}, u32[]{:S(2)}) collective-permute-start(f32[1,256]{1,0:T(1,128)S(1)} %get-tuple-element.45), channel_id=1, source_target_pairs={{0,8},{1,9},{2,10},{3,11},{4,12},{5,13},{6,14},{7,15},{8,16},{9,17... | collective-permute-start | bytes 3080 | tf_op jit(solution)/shard_map/ppermute | solution.py:194
  53.6 4.8 %collective-permute-start.13 = (f32[1,256]{1,0:T(1,128)S(1)}, f32[1,256]{1,0:T(1,128)S(1)}, u32[]{:S(2)}, u32[]{:S(2)}) collective-permute-start(f32[1,256]{1,0:T(1,128)S(1)} %get-tuple-element.46), channel_id=1, source_target_pairs={{0,4},{1,5},{2,6},{3,7},{4,8},{5,9},{6,10},{7,11},{8,12},{9,13},{1... | collective-permute-start | bytes 3080 | tf_op jit(solution)/shard_map/ppermute | solution.py:194

commit v2 on v1

--- a/solution.py
+++ b/solution.py
@@ -8,7 +8,7 @@
 SIZES = (2, 8, 4)
 SENDS = [((0,), (0, 2, 0)), ((0,), (1, 0, 1)), ((0,), (0, 0, -1)), ((0,), (0, 0, 1)), ((0,), (0, 1, 0)), ((1,), (0, 1, 0)), ((4,), (0, 0, 1)), ((3,), (1, 0, 0)), ((2,), (0, 0, 1)), ((2,), (0, 0, -1)), ((6,), (0, 1, 0))]
 ROWS = [6, 1, 5]
-STAGES = [[(1, 0), (2, 0), (2, 1), (3, 0), (3, 1), (3, 2), (4, 1), (4, 2), (4, 3), (5, 0), (5, 2), (5, 3), (5, 4)], [(6, 0), (6, 2), (6, 3), (6, 4), (7, 1), (7, 5), (7, 6), (8, 1), (8, 5), (8, 6)], [(11, 0), (11, 2), (11, 3), (11, 4), (11, 7), (11, 8), (11, 9), (11, 10), (9, 1), (9, 5), (9, 6), (10, 1), (10, 5), (10, 6)]]
+STAGES = [[(1, 0), (2, 0), (2, 1), (3, 0), (3, 1), (3, 2), (4, 1), (4, 2), (4, 3), (5, 0), (5, 2), (5, 3), (5, 4)], [(6, 0), (6, 2), (6, 3), (6, 4), (7, 1), (7, 5), (7, 6), (8, 1), (8, 5), (8, 6)], [(10, 1), (10, 5), (10, 6)], [(11, 0), (11, 2), (11, 3), (11, 4), (11, 7), (11, 8), (11, 9), (11, 10), (9, 1), (9, 5), (9, 6)]]
 FIRST = 6
 HELD = (1,)
 BOTH = ("clusters", "members")

time: 59.1 us -> 58.7 us (level)
  starting transfers between devices: 37.2 us -> 35.9 us
  Pallas kernels: 9.75 us -> 10.6 us
    all_to_all x1, starting transfers between devices: 7.22 us -> 5.9 us  [per_device(): lax.all_to_all(best, 'members', 0, 0, axis_index_groups=plane_groups(memb...]
    pallas_call x5 -> x6, Pallas kernels: 7.8 us -> 8.64 us  [call_kernel(): pl.pallas_call(kernel, out_shape=[jax.ShapeDtypeStruct(one, jnp.float32)...]
  transfers between devices with their start and end apart: 15 -> 15, of which waited for: 5 -> 5; matrix products, arithmetic and copies ran while one was open for 0% -> 0% of each run, Pallas kernels for 10% -> 12%
where the time goes in v2:
time: 58.7 us; the launch traced here: 58.5 us
  starting transfers between devices  35.9 us (61%)
  waiting for transfers between devices  11 us (19%)
  Pallas kernels  10.6 us (18%)
  local copies, waits for them, and re-layouts  0.91 us (2%)
    ppermute x11, starting transfers between devices, per_device(): lax.ppermute(blocks[slot], BOTH, shift_pairs(shift, False, clusters, memb...  23.1 us
    pallas_call x6, Pallas kernels, call_kernel(): pl.pallas_call(kernel, out_shape=[jax.ShapeDtypeStruct(one, jnp.float32)...  8.64 us
    ppermute x11, waiting for transfers between devices, per_device(): lax.ppermute(blocks[slot], BOTH, shift_pairs(shift, False, clusters, memb...  7.09 us
    ppermute x3, starting transfers between devices, per_device(): lax.ppermute(row, BOTH, shift_pairs(places[slot], True, clusters, members))  6.95 us
    all_to_all x1, starting transfers between devices, per_device(): lax.all_to_all(best, 'members', 0, 0, axis_index_groups=plane_groups(memb...  5.9 us
    ppermute x3, waiting for transfers between devices, per_device(): lax.ppermute(row, BOTH, shift_pairs(places[slot], True, clusters, members))  3.88 us
    pallas_call x12, Pallas kernels, normalize(): pl.pallas_call(normalize_kernel, out_shape=jax.ShapeDtypeStruct(embedding...  1.95 us
  transfers between devices with their start and end apart: 15, of which 5 were waited for; matrix products, arithmetic and copies ran while one was open for 0% of the time, Pallas kernels for 12%

profile of v2, /device:TPU:6, one launch (start us, length us, event | category | flops | bytes accessed | tf_op | source)
XLA Modules:
  0.0 58.5 jit_solution(16993205679984161261)
XLA Ops:
  0.0 0.0 copy-start
  0.0 6.3 %collective-permute-start = (bf16[256,768]{1,0:T(8,128)(2,1)}, bf16[256,768]{1,0:T(8,128)(2,1)S(1)}, u32[]{:S(2)}, u32[]{:S(2)}) collective-permute-start(bf16[256,768]{1,0:T(8,128)(2,1)} %x_ref.1), channel_id=1, source_target_pairs={{8,0},{9,1},{10,2},{11,3},{12,4},{13,5},{14,6},{15,7},{16,8},{17,9... | collective-permute-start | bytes 1179656 | tf_op jit(solution)/shard_map/ppermute | solution.py:190
  6.3 1.6 %collective-permute-start.2 = (bf16[256,768]{1,0:T(8,128)(2,1)}, bf16[256,768]{1,0:T(8,128)(2,1)S(1)}, u32[]{:S(2)}, u32[]{:S(2)}) collective-permute-start(bf16[256,768]{1,0:T(8,128)(2,1)} %x_ref.1), channel_id=1, source_target_pairs={{3,0},{0,1},{1,2},{2,3},{7,4},{4,5},{5,6},{6,7},{11,8},{8,9},{9,10... | collective-permute-start | bytes 1179656 | tf_op jit(solution)/shard_map/ppermute | solution.py:190
  7.9 1.7 %collective-permute-start.3 = (bf16[256,768]{1,0:T(8,128)(2,1)}, bf16[256,768]{1,0:T(8,128)(2,1)S(1)}, u32[]{:S(2)}, u32[]{:S(2)}) collective-permute-start(bf16[256,768]{1,0:T(8,128)(2,1)} %x_ref.1), channel_id=1, source_target_pairs={{1,0},{2,1},{3,2},{0,3},{5,4},{6,5},{7,6},{4,7},{9,8},{10,9},{11,1... | collective-permute-start | bytes 1179656 | tf_op jit(solution)/shard_map/ppermute | solution.py:190
  9.5 2.6 %collective-permute-start.1 = (bf16[256,768]{1,0:T(8,128)(2,1)}, bf16[256,768]{1,0:T(8,128)(2,1)S(1)}, u32[]{:S(2)}, u32[]{:S(2)}) collective-permute-start(bf16[256,768]{1,0:T(8,128)(2,1)} %x_ref.1), channel_id=1, source_target_pairs={{33,0},{34,1},{35,2},{32,3},{37,4},{38,5},{39,6},{36,7},{41,8},{42... | collective-permute-start | bytes 1179656 | tf_op jit(solution)/shard_map/ppermute | solution.py:190
  12.2 1.0 %collective-permute-start.4 = (bf16[256,768]{1,0:T(8,128)(2,1)}, bf16[256,768]{1,0:T(8,128)(2,1)S(1)}, u32[]{:S(2)}, u32[]{:S(2)}) collective-permute-start(bf16[256,768]{1,0:T(8,128)(2,1)} %x_ref.1), channel_id=1, source_target_pairs={{4,0},{5,1},{6,2},{7,3},{8,4},{9,5},{10,6},{11,7},{12,8},{13,9},{1... | collective-permute-start | bytes 1179656 | tf_op jit(solution)/shard_map/ppermute | solution.py:190
  13.2 0.0 copy-start.1
  13.2 0.7 %copy-done.1 = s32[256]{0:T(256)S(1)} copy-done((s32[256]{0:T(256)S(1)}, s32[256]{0:T(256)}, u32[]{:S(2)}) %copy-start.1) | copy-done | bytes 1048
  13.9 0.1 copy.3.column_ref
  14.0 0.1 stack.51.refs_0_
  14.1 0.0 copy-done
  14.1 0.2 shard_map.28.unit_ref.refs_1_
  14.3 0.3 shard_map.29.refs_7_
  14.6 1.6 %collective-permute-done.x_ref = bf16[256,768]{1,0:T(8,128)(2,1)S(1)} collective-permute-done((bf16[256,768]{1,0:T(8,128)(2,1)}, bf16[256,768]{1,0:T(8,128)(2,1)S(1)}, u32[]{:S(2)}, u32[]{:S(2)}) %collective-permute-start) | collective-permute-done | bytes 393248 | tf_op jit(solution)/shard_map/ppermute | solution.py:190
  16.2 2.7 %collective-permute-start.5 = (bf16[256,768]{1,0:T(8,128)(2,1)S(1)}, bf16[256,768]{1,0:T(8,128)(2,1)S(1)}, u32[]{:S(2)}, u32[]{:S(2)}) collective-permute-start(bf16[256,768]{1,0:T(8,128)(2,1)S(1)} %collective-permute-done.x_ref), channel_id=1, source_target_pairs={{4,0},{5,1},{6,2},{7,3},{8,4},{9,5},{10,6},{11,7},{12,8},{13,9},{1... | collective-permute-start | bytes 1179656 | tf_op jit(solution)/shard_map/ppermute | solution.py:190
  18.8 3.4 %collective-permute-done.2.x_ref = bf16[256,768]{1,0:T(8,128)(2,1)S(1)} collective-permute-done((bf16[256,768]{1,0:T(8,128)(2,1)}, bf16[256,768]{1,0:T(8,128)(2,1)S(1)}, u32[]{:S(2)}, u32[]{:S(2)}) %collective-permute-start.2) | collective-permute-done | bytes 393248 | tf_op jit(solution)/shard_map/ppermute | solution.py:190
  22.2 1.4 %collective-permute-start.7 = (bf16[256,768]{1,0:T(8,128)(2,1)S(1)}, bf16[256,768]{1,0:T(8,128)(2,1)S(1)}, u32[]{:S(2)}, u32[]{:S(2)}) collective-permute-start(bf16[256,768]{1,0:T(8,128)(2,1)S(1)} %collective-permute-done.2.x_ref), channel_id=1, source_target_pairs={{32,0},{33,1},{34,2},{35,3},{36,4},{37,5},{38,6},{39,7},{40,8},{41... | collective-permute-start | bytes 1179656 | tf_op jit(solution)/shard_map/ppermute | solution.py:190
  23.6 0.0 collective-permute-done.3.x_ref
  23.6 0.0 collective-permute-start.6
  23.6 0.0 collective-permute-done.1.x_ref
  23.6 2.0 %collective-permute-start.10 = (bf16[256,768]{1,0:T(8,128)(2,1)S(1)}, bf16[256,768]{1,0:T(8,128)(2,1)S(1)}, u32[]{:S(2)}, u32[]{:S(2)}) collective-permute-start(bf16[256,768]{1,0:T(8,128)(2,1)S(1)} %collective-permute-done.1.x_ref), channel_id=1, source_target_pairs={{3,0},{0,1},{1,2},{2,3},{7,4},{4,5},{5,6},{6,7},{11,8},{8,9},{9,10... | collective-permute-start | bytes 1179656 | tf_op jit(solution)/shard_map/ppermute | solution.py:190
  25.7 0.0 collective-permute-done.4.x_ref
  25.7 1.3 %collective-permute-start.8 = (bf16[256,768]{1,0:T(8,128)(2,1)S(1)}, bf16[256,768]{1,0:T(8,128)(2,1)S(1)}, u32[]{:S(2)}, u32[]{:S(2)}) collective-permute-start(bf16[256,768]{1,0:T(8,128)(2,1)S(1)} %collective-permute-done.1.x_ref), channel_id=1, source_target_pairs={{1,0},{2,1},{3,2},{0,3},{5,4},{6,5},{7,6},{4,7},{9,8},{10,9},{11,1... | collective-permute-start | bytes 1179656 | tf_op jit(solution)/shard_map/ppermute | solution.py:190
  27.0 0.0 collective-permute-done.5.x_ref
  27.0 2.5 %collective-permute-start.9 = (bf16[256,768]{1,0:T(8,128)(2,1)S(1)}, bf16[256,768]{1,0:T(8,128)(2,1)S(1)}, u32[]{:S(2)}, u32[]{:S(2)}) collective-permute-start(bf16[256,768]{1,0:T(8,128)(2,1)S(1)} %collective-permute-done.5.x_ref), channel_id=1, source_target_pairs={{4,0},{5,1},{6,2},{7,3},{8,4},{9,5},{10,6},{11,7},{12,8},{13,9},{1... | collective-permute-start | bytes 1179656 | tf_op jit(solution)/shard_map/ppermute | solution.py:190
  29.5 0.2 shard_map.30.refs_2_.refs_1_
  29.6 0.2 shard_map.34.refs_6_.refs_2_
  29.8 0.2 shard_map.31.refs_3_
  29.9 0.2 shard_map.32.refs_4_
  30.1 0.2 shard_map.33.refs_5_
  30.3 2.2 %shard_map.35.refs_10_ = f32[12,8,256]{2,1,0:T(8,128)S(1)} custom-call(s32[12]{0:T(128)S(1)} %stack.51.refs_0_, bf16[256,768]{1,0:T(8,128)(2,1)S(1)} %shard_map.28.unit_ref.refs_1_, bf16[256,768]{1,0:T(8,128)(2,1)S(1)} %shard_map.30.refs_2_.refs_1_, bf16[256,768]{1,0:T(8,128)(2,1)S(1)} %shard_map.31.refs_3_, bf16[256,768]{1,0:T(8,128)(2,1)S(1)} %shard_map.32.refs_4_, ...), custom_call_target="tpu_custom_call" | custom-call | flops 1308622848 | bytes 5111808 | tf_op jit(solution)/shard_map/pallas_call | solution.py:130
  32.5 0.0 collective-permute-done.7.x_ref
  32.5 0.0 collective-permute-done.6.x_ref
  32.5 0.2 shard_map.36.refs_7_.refs_3_
  32.7 0.2 shard_map.37.refs_8_
  32.8 0.2 shard_map.38.refs_9_
  33.0 1.9 %shard_map.39.refs_5_ = f32[12,8,256]{2,1,0:T(8,128)S(1)} custom-call(s32[12]{0:T(128)S(1)} %stack.51.refs_0_, bf16[256,768]{1,0:T(8,128)(2,1)S(1)} %shard_map.28.unit_ref.refs_1_, bf16[256,768]{1,0:T(8,128)(2,1)S(1)} %shard_map.30.refs_2_.refs_1_, bf16[256,768]{1,0:T(8,128)(2,1)S(1)} %shard_map.31.refs_3_, bf16[256,768]{1,0:T(8,128)(2,1)S(1)} %shard_map.32.refs_4_, ...), custom_call_target="tpu_custom_call" | custom-call | flops 1006632960 | bytes 3932160 | tf_op jit(solution)/shard_map/pallas_call | solution.py:130
  34.9 2.1 %collective-permute-done.10.x_ref = bf16[256,768]{1,0:T(8,128)(2,1)S(1)} collective-permute-done((bf16[256,768]{1,0:T(8,128)(2,1)S(1)}, bf16[256,768]{1,0:T(8,128)(2,1)S(1)}, u32[]{:S(2)}, u32[]{:S(2)}) %collective-permute-start.10) | collective-permute-done | bytes 393248 | tf_op jit(solution)/shard_map/ppermute | solution.py:190
  37.0 0.2 shard_map.40.refs_4_.refs_11_
  37.1 1.1 %shard_map.41.refs_13_ = f32[12,8,256]{2,1,0:T(8,128)S(1)} custom-call(s32[12]{0:T(128)S(1)} %stack.51.refs_0_, bf16[256,768]{1,0:T(8,128)(2,1)S(1)} %shard_map.30.refs_2_.refs_1_, bf16[256,768]{1,0:T(8,128)(2,1)S(1)} %shard_map.34.refs_6_.refs_2_, bf16[256,768]{1,0:T(8,128)(2,1)S(1)} %shard_map.36.refs_7_.refs_3_, ...), custom_call_target="tpu_custom_call" | custom-call | flops 301989888 | bytes 1179648 | tf_op jit(solution)/shard_map/pallas_call | solution.py:130
  38.3 0.0 collective-permute-done.8.x_ref
  38.3 0.0 collective-permute-done.9.x_ref
  38.3 0.2 shard_map.42.refs_10_
  38.5 0.2 shard_map.43.refs_12_
  38.6 2.6 %shard_map.44 = (f32[8,1,256]{2,1,0:T(1,128)}, f32[1,256]{1,0:T(1,128)S(1)}, f32[1,256]{1,0:T(1,128)S(1)}, f32[1,256]{1,0:T(1,128)S(1)}) custom-call(s32[12]{0:T(128)S(1)} %stack.51.refs_0_, bf16[256,768]{1,0:T(8,128)(2,1)S(1)} %shard_map.28.unit_ref.refs_1_, bf16[256,768]{1,0:T(8,128)(2,1)S(1)} %shard_map.30.refs_2_.refs_1_, ...), custom_call_target="tpu_custom_call" | custom-call | flops 1107296256 | bytes 4325376 | tf_op jit(solution)/shard_map/pallas_call | solution.py:130
  41.2 5.9 %all-to-all-start = ((f32[8,1,256]{2,1,0:T(1,128)}), f32[8,1,256]{2,1,0:T(1,128)S(1)}, u32[]{:S(2)}, u32[]{:S(2)}) async-start(f32[8,1,256]{2,1,0:T(1,128)} %get-tuple-element.45), calls=%async_computation | async-start | bytes 16384 | tf_op jit(solution)/shard_map/all_to_all | solution.py:197
  47.1 1.5 %collective-permute-start.11 = (f32[1,256]{1,0:T(1,128)S(1)}, f32[1,256]{1,0:T(1,128)S(1)}, u32[]{:S(2)}, u32[]{:S(2)}) collective-permute-start(f32[1,256]{1,0:T(1,128)S(1)} %get-tuple-element.46), channel_id=1, source_target_pairs={{0,12},{1,13},{2,14},{3,15},{4,16},{5,17},{6,18},{7,19},{8,20},{9,... | collective-permute-start | bytes 3080 | tf_op jit(solution)/shard_map/ppermute | solution.py:194
  48.6 4.6 %collective-permute-start.12 = (f32[1,256]{1,0:T(1,128)S(1)}, f32[1,256]{1,0:T(1,128)S(1)}, u32[]{:S(2)}, u32[]{:S(2)}) collective-permute-start(f32[1,256]{1,0:T(1,128)S(1)} %get-tuple-element.47), channel_id=1, source_target_pairs={{0,8},{1,9},{2,10},{3,11},{4,12},{5,13},{6,14},{7,15},{8,16},{9,17... | collective-permute-start | bytes 3080 | tf_op jit(solution)/shard_map/ppermute | solution.py:194
  53.2 0.9 %collective-permute-start.13 = (f32[1,256]{1,0:T(1,128)S(1)}, f32[1,256]{1,0:T(1,128)S(1)}, u32[]{:S(2)}, u32[]{:S(2)}) collective-permute-start(f32[1,256]{1,0:T(1,128)S(1)} %get-tuple-element.48), channel_id=1, source_target_pairs={{0,4},{1,5},{2,6},{3,7},{4,8},{5,9},{6,10},{7,11},{8,12},{9,13},{1... | collective-permute-start | bytes 3080 | tf_op jit(solution)/shard_map/ppermute | solution.py:194
  54.1 0.0 collective-permute-done.11.refs_0_
  54.1 1.1 %collective-permute-done.12.refs_1_ = f32[1,256]{1,0:T(1,128)S(1)} collective-permute-done((f32[1,256]{1,0:T(1,128)S(1)}, f32[1,256]{1,0:T(1,128)S(1)}, u32[]{:S(2)}, u32[]{:S(2)}) %collective-permute-start.12) | collective-permute-done | bytes 1056 | tf_op jit(solution)/shard_map/ppermute | solution.py:194
  55.2 2.8 %collective-permute-done.13.refs_2_ = f32[1,256]{1,0:T(1,128)S(1)} collective-permute-done((f32[1,256]{1,0:T(1,128)S(1)}, f32[1,256]{1,0:T(1,128)S(1)}, u32[]{:S(2)}, u32[]{:S(2)}) %collective-permute-start.13) | collective-permute-done | bytes 1056 | tf_op jit(solution)/shard_map/ppermute | solution.py:194
  57.9 0.0 all-to-all-done.found_ref
  57.9 0.6 shard_map.45
Async XLA Ops:
  0.0 14.1 %copy-start = (bf16[256,768]{1,0:T(8,128)(2,1)S(1)}, bf16[256,768]{1,0:T(8,128)(2,1)}, u32[]{:S(2)}) copy-start(bf16[256,768]{1,0:T(8,128)(2,1)} %x_ref.1) | copy-start | bytes 1179652
  0.0 16.2 %collective-permute-start = (bf16[256,768]{1,0:T(8,128)(2,1)}, bf16[256,768]{1,0:T(8,128)(2,1)S(1)}, u32[]{:S(2)}, u32[]{:S(2)}) collective-permute-start(bf16[256,768]{1,0:T(8,128)(2,1)} %x_ref.1), channel_id=1, source_target_pairs={{8,0},{9,1},{10,2},{11,3},{12,4},{13,5},{14,6},{15,7},{16,8},{17,9... | collective-permute-start | bytes 1179656 | tf_op jit(solution)/shard_map/ppermute | solution.py:190
  6.3 15.9 %collective-permute-start.2 = (bf16[256,768]{1,0:T(8,128)(2,1)}, bf16[256,768]{1,0:T(8,128)(2,1)S(1)}, u32[]{:S(2)}, u32[]{:S(2)}) collective-permute-start(bf16[256,768]{1,0:T(8,128)(2,1)} %x_ref.1), channel_id=1, source_target_pairs={{3,0},{0,1},{1,2},{2,3},{7,4},{4,5},{5,6},{6,7},{11,8},{8,9},{9,10... | collective-permute-start | bytes 1179656 | tf_op jit(solution)/shard_map/ppermute | solution.py:190
  7.9 15.7 %collective-permute-start.3 = (bf16[256,768]{1,0:T(8,128)(2,1)}, bf16[256,768]{1,0:T(8,128)(2,1)S(1)}, u32[]{:S(2)}, u32[]{:S(2)}) collective-permute-start(bf16[256,768]{1,0:T(8,128)(2,1)} %x_ref.1), channel_id=1, source_target_pairs={{1,0},{2,1},{3,2},{0,3},{5,4},{6,5},{7,6},{4,7},{9,8},{10,9},{11,1... | collective-permute-start | bytes 1179656 | tf_op jit(solution)/shard_map/ppermute | solution.py:190
  9.5 14.1 %collective-permute-start.1 = (bf16[256,768]{1,0:T(8,128)(2,1)}, bf16[256,768]{1,0:T(8,128)(2,1)S(1)}, u32[]{:S(2)}, u32[]{:S(2)}) collective-permute-start(bf16[256,768]{1,0:T(8,128)(2,1)} %x_ref.1), channel_id=1, source_target_pairs={{33,0},{34,1},{35,2},{32,3},{37,4},{38,5},{39,6},{36,7},{41,8},{42... | collective-permute-start | bytes 1179656 | tf_op jit(solution)/shard_map/ppermute | solution.py:190
  12.2 13.5 %collective-permute-start.4 = (bf16[256,768]{1,0:T(8,128)(2,1)}, bf16[256,768]{1,0:T(8,128)(2,1)S(1)}, u32[]{:S(2)}, u32[]{:S(2)}) collective-permute-start(bf16[256,768]{1,0:T(8,128)(2,1)} %x_ref.1), channel_id=1, source_target_pairs={{4,0},{5,1},{6,2},{7,3},{8,4},{9,5},{10,6},{11,7},{12,8},{13,9},{1... | collective-permute-start | bytes 1179656 | tf_op jit(solution)/shard_map/ppermute | solution.py:190
  13.2 0.7 %copy-start.1 = (s32[256]{0:T(256)S(1)}, s32[256]{0:T(256)}, u32[]{:S(2)}) copy-start(s32[256]{0:T(256)} %param.3) | copy-start | bytes 3076
  16.2 10.8 %collective-permute-start.5 = (bf16[256,768]{1,0:T(8,128)(2,1)S(1)}, bf16[256,768]{1,0:T(8,128)(2,1)S(1)}, u32[]{:S(2)}, u32[]{:S(2)}) collective-permute-start(bf16[256,768]{1,0:T(8,128)(2,1)S(1)} %collective-permute-done.x_ref), channel_id=1, source_target_pairs={{4,0},{5,1},{6,2},{7,3},{8,4},{9,5},{10,6},{11,7},{12,8},{13,9},{1... | collective-permute-start | bytes 1179656 | tf_op jit(solution)/shard_map/ppermute | solution.py:190
  22.2 10.3 %collective-permute-start.7 = (bf16[256,768]{1,0:T(8,128)(2,1)S(1)}, bf16[256,768]{1,0:T(8,128)(2,1)S(1)}, u32[]{:S(2)}, u32[]{:S(2)}) collective-permute-start(bf16[256,768]{1,0:T(8,128)(2,1)S(1)} %collective-permute-done.2.x_ref), channel_id=1, source_target_pairs={{32,0},{33,1},{34,2},{35,3},{36,4},{37,5},{38,6},{39,7},{40,8},{41... | collective-permute-start | bytes 1179656 | tf_op jit(solution)/shard_map/ppermute | solution.py:190
  23.6 8.9 %collective-permute-start.6 = (bf16[256,768]{1,0:T(8,128)(2,1)S(1)}, bf16[256,768]{1,0:T(8,128)(2,1)S(1)}, u32[]{:S(2)}, u32[]{:S(2)}) collective-permute-start(bf16[256,768]{1,0:T(8,128)(2,1)S(1)} %collective-permute-done.3.x_ref), channel_id=1, source_target_pairs={{1,0},{2,1},{3,2},{0,3},{5,4},{6,5},{7,6},{4,7},{9,8},{10,9},{11,1... | collective-permute-start | bytes 1179656 | tf_op jit(solution)/shard_map/ppermute | solution.py:190
  23.6 13.3 %collective-permute-start.10 = (bf16[256,768]{1,0:T(8,128)(2,1)S(1)}, bf16[256,768]{1,0:T(8,128)(2,1)S(1)}, u32[]{:S(2)}, u32[]{:S(2)}) collective-permute-start(bf16[256,768]{1,0:T(8,128)(2,1)S(1)} %collective-permute-done.1.x_ref), channel_id=1, source_target_pairs={{3,0},{0,1},{1,2},{2,3},{7,4},{4,5},{5,6},{6,7},{11,8},{8,9},{9,10... | collective-permute-start | bytes 1179656 | tf_op jit(solution)/shard_map/ppermute | solution.py:190
  25.7 12.6 %collective-permute-start.8 = (bf16[256,768]{1,0:T(8,128)(2,1)S(1)}, bf16[256,768]{1,0:T(8,128)(2,1)S(1)}, u32[]{:S(2)}, u32[]{:S(2)}) collective-permute-start(bf16[256,768]{1,0:T(8,128)(2,1)S(1)} %collective-permute-done.1.x_ref), channel_id=1, source_target_pairs={{1,0},{2,1},{3,2},{0,3},{5,4},{6,5},{7,6},{4,7},{9,8},{10,9},{11,1... | collective-permute-start | bytes 1179656 | tf_op jit(solution)/shard_map/ppermute | solution.py:190
  27.0 11.3 %collective-permute-start.9 = (bf16[256,768]{1,0:T(8,128)(2,1)S(1)}, bf16[256,768]{1,0:T(8,128)(2,1)S(1)}, u32[]{:S(2)}, u32[]{:S(2)}) collective-permute-start(bf16[256,768]{1,0:T(8,128)(2,1)S(1)} %collective-permute-done.5.x_ref), channel_id=1, source_target_pairs={{4,0},{5,1},{6,2},{7,3},{8,4},{9,5},{10,6},{11,7},{12,8},{13,9},{1... | collective-permute-start | bytes 1179656 | tf_op jit(solution)/shard_map/ppermute | solution.py:190
  41.2 16.7 %all-to-all-start = ((f32[8,1,256]{2,1,0:T(1,128)}), f32[8,1,256]{2,1,0:T(1,128)S(1)}, u32[]{:S(2)}, u32[]{:S(2)}) async-start(f32[8,1,256]{2,1,0:T(1,128)} %get-tuple-element.45), calls=%async_computation | async-start | bytes 16384 | tf_op jit(solution)/shard_map/all_to_all | solution.py:197
  47.1 7.0 %collective-permute-start.11 = (f32[1,256]{1,0:T(1,128)S(1)}, f32[1,256]{1,0:T(1,128)S(1)}, u32[]{:S(2)}, u32[]{:S(2)}) collective-permute-start(f32[1,256]{1,0:T(1,128)S(1)} %get-tuple-element.46), channel_id=1, source_target_pairs={{0,12},{1,13},{2,14},{3,15},{4,16},{5,17},{6,18},{7,19},{8,20},{9,... | collective-permute-start | bytes 3080 | tf_op jit(solution)/shard_map/ppermute | solution.py:194
  48.6 6.6 %collective-permute-start.12 = (f32[1,256]{1,0:T(1,128)S(1)}, f32[1,256]{1,0:T(1,128)S(1)}, u32[]{:S(2)}, u32[]{:S(2)}) collective-permute-start(f32[1,256]{1,0:T(1,128)S(1)} %get-tuple-element.47), channel_id=1, source_target_pairs={{0,8},{1,9},{2,10},{3,11},{4,12},{5,13},{6,14},{7,15},{8,16},{9,17... | collective-permute-start | bytes 3080 | tf_op jit(solution)/shard_map/ppermute | solution.py:194
  53.2 4.8 %collective-permute-start.13 = (f32[1,256]{1,0:T(1,128)S(1)}, f32[1,256]{1,0:T(1,128)S(1)}, u32[]{:S(2)}, u32[]{:S(2)}) collective-permute-start(f32[1,256]{1,0:T(1,128)S(1)} %get-tuple-element.48), channel_id=1, source_target_pairs={{0,4},{1,5},{2,6},{3,7},{4,8},{5,9},{6,10},{7,11},{8,12},{9,13},{1... | collective-permute-start | bytes 3080 | tf_op jit(solution)/shard_map/ppermute | solution.py:194

commit v3 on v2

--- a/solution.py
+++ b/solution.py
@@ -8,7 +8,7 @@
 SIZES = (2, 8, 4)
 SENDS = [((0,), (0, 2, 0)), ((0,), (1, 0, 1)), ((0,), (0, 0, -1)), ((0,), (0, 0, 1)), ((0,), (0, 1, 0)), ((1,), (0, 1, 0)), ((4,), (0, 0, 1)), ((3,), (1, 0, 0)), ((2,), (0, 0, 1)), ((2,), (0, 0, -1)), ((6,), (0, 1, 0))]
 ROWS = [6, 1, 5]
-STAGES = [[(1, 0), (2, 0), (2, 1), (3, 0), (3, 1), (3, 2), (4, 1), (4, 2), (4, 3), (5, 0), (5, 2), (5, 3), (5, 4)], [(6, 0), (6, 2), (6, 3), (6, 4), (7, 1), (7, 5), (7, 6), (8, 1), (8, 5), (8, 6)], [(10, 1), (10, 5), (10, 6)], [(11, 0), (11, 2), (11, 3), (11, 4), (11, 7), (11, 8), (11, 9), (11, 10), (9, 1), (9, 5), (9, 6)]]
+STAGES = [[(1, 0), (2, 0), (2, 1), (3, 0), (3, 1), (3, 2), (4, 1), (4, 2), (4, 3), (5, 0), (5, 2), (5, 3), (5, 4)], [(6, 0), (6, 2), (6, 3), (6, 4), (7, 1), (7, 5), (7, 6), (8, 1), (8, 5), (8, 6)], [(10, 1), (10, 5), (10, 6)], [(11, 0), (11, 2), (11, 3), (11, 4), (11, 7), (11, 8), (11, 10)], [(11, 9), (9, 1), (9, 5), (9, 6)]]
 FIRST = 6
 HELD = (1,)
 BOTH = ("clusters", "members")

time: 58.7 us -> 59 us (level)
  waiting for transfers between devices: 11 us -> 9.8 us
  Pallas kernels: 10.6 us -> 11.4 us
  starting transfers between devices: 35.9 us -> 36.6 us
    ppermute x11, starting transfers between devices: 23.1 us -> 26.1 us  [per_device(): lax.ppermute(blocks[slot], BOTH, shift_pairs(shift, False, clusters, memb...]
    ppermute x3, starting transfers between devices: 6.95 us -> 5.21 us  [per_device(): lax.ppermute(row, BOTH, shift_pairs(places[slot], True, clusters, members))]
    ppermute x11, waiting for transfers between devices: 7.09 us -> 5.55 us  [per_device(): lax.ppermute(blocks[slot], BOTH, shift_pairs(shift, False, clusters, memb...]
    pallas_call x6 -> x7, Pallas kernels: 8.64 us -> 9.44 us  [call_kernel(): pl.pallas_call(kernel, out_shape=[jax.ShapeDtypeStruct(one, jnp.float32)...]
    all_to_all x1, starting transfers between devices: 5.9 us -> 5.23 us  [per_device(): lax.all_to_all(best, 'members', 0, 0, axis_index_groups=plane_groups(memb...]
  transfers between devices with their start and end apart: 15 -> 15, of which waited for: 5 -> 7; matrix products, arithmetic and copies ran while one was open for 0% -> 0% of each run, Pallas kernels for 12% -> 15%
where the time goes in v3:
time: 59 us; the launch traced here: 58.8 us
  starting transfers between devices  36.6 us (62%)
  Pallas kernels  11.4 us (19%)
  waiting for transfers between devices  9.8 us (17%)
  local copies, waits for them, and re-layouts  0.91 us (2%)
    ppermute x11, starting transfers between devices, per_device(): lax.ppermute(blocks[slot], BOTH, shift_pairs(shift, False, clusters, memb...  26.1 us
    pallas_call x7, Pallas kernels, call_kernel(): pl.pallas_call(kernel, out_shape=[jax.ShapeDtypeStruct(one, jnp.float32)...  9.44 us
    ppermute x11, waiting for transfers between devices, per_device(): lax.ppermute(blocks[slot], BOTH, shift_pairs(shift, False, clusters, memb...  5.55 us
    all_to_all x1, starting transfers between devices, per_device(): lax.all_to_all(best, 'members', 0, 0, axis_index_groups=plane_groups(memb...  5.23 us
    ppermute x3, starting transfers between devices, per_device(): lax.ppermute(row, BOTH, shift_pairs(places[slot], True, clusters, members))  5.21 us
    ppermute x3, waiting for transfers between devices, per_device(): lax.ppermute(row, BOTH, shift_pairs(places[slot], True, clusters, members))  4.24 us
    pallas_call x12, Pallas kernels, normalize(): pl.pallas_call(normalize_kernel, out_shape=jax.ShapeDtypeStruct(embedding...  1.95 us
  transfers between devices with their start and end apart: 15, of which 7 were waited for; matrix products, arithmetic and copies ran while one was open for 0% of the time, Pallas kernels for 15%

profile of v3, /device:TPU:6, one launch (start us, length us, event | category | flops | bytes accessed | tf_op | source)
XLA Modules:
  0.0 58.8 jit_solution(9883918998132464870)
XLA Ops:
  0.0 0.0 copy-start
  0.0 6.3 %collective-permute-start = (bf16[256,768]{1,0:T(8,128)(2,1)}, bf16[256,768]{1,0:T(8,128)(2,1)S(1)}, u32[]{:S(2)}, u32[]{:S(2)}) collective-permute-start(bf16[256,768]{1,0:T(8,128)(2,1)} %x_ref.1), channel_id=1, source_target_pairs={{8,0},{9,1},{10,2},{11,3},{12,4},{13,5},{14,6},{15,7},{16,8},{17,9... | collective-permute-start | bytes 1179656 | tf_op jit(solution)/shard_map/ppermute | solution.py:190
  6.3 1.6 %collective-permute-start.2 = (bf16[256,768]{1,0:T(8,128)(2,1)}, bf16[256,768]{1,0:T(8,128)(2,1)S(1)}, u32[]{:S(2)}, u32[]{:S(2)}) collective-permute-start(bf16[256,768]{1,0:T(8,128)(2,1)} %x_ref.1), channel_id=1, source_target_pairs={{3,0},{0,1},{1,2},{2,3},{7,4},{4,5},{5,6},{6,7},{11,8},{8,9},{9,10... | collective-permute-start | bytes 1179656 | tf_op jit(solution)/shard_map/ppermute | solution.py:190
  7.9 1.7 %collective-permute-start.3 = (bf16[256,768]{1,0:T(8,128)(2,1)}, bf16[256,768]{1,0:T(8,128)(2,1)S(1)}, u32[]{:S(2)}, u32[]{:S(2)}) collective-permute-start(bf16[256,768]{1,0:T(8,128)(2,1)} %x_ref.1), channel_id=1, source_target_pairs={{1,0},{2,1},{3,2},{0,3},{5,4},{6,5},{7,6},{4,7},{9,8},{10,9},{11,1... | collective-permute-start | bytes 1179656 | tf_op jit(solution)/shard_map/ppermute | solution.py:190
  9.5 2.6 %collective-permute-start.1 = (bf16[256,768]{1,0:T(8,128)(2,1)}, bf16[256,768]{1,0:T(8,128)(2,1)S(1)}, u32[]{:S(2)}, u32[]{:S(2)}) collective-permute-start(bf16[256,768]{1,0:T(8,128)(2,1)} %x_ref.1), channel_id=1, source_target_pairs={{33,0},{34,1},{35,2},{32,3},{37,4},{38,5},{39,6},{36,7},{41,8},{42... | collective-permute-start | bytes 1179656 | tf_op jit(solution)/shard_map/ppermute | solution.py:190
  12.2 0.0 copy-start.1
  12.2 0.7 %copy-done.1 = s32[256]{0:T(256)S(1)} copy-done((s32[256]{0:T(256)S(1)}, s32[256]{0:T(256)}, u32[]{:S(2)}) %copy-start.1) | copy-done | bytes 1048
  12.9 0.1 copy.3.column_ref
  13.0 0.1 stack.51.refs_0_
  13.1 0.0 copy-done
  13.1 0.2 shard_map.28.unit_ref.refs_1_
  13.3 0.3 shard_map.29.refs_7_
  13.6 2.6 %collective-permute-done.x_ref = bf16[256,768]{1,0:T(8,128)(2,1)S(1)} collective-permute-done((bf16[256,768]{1,0:T(8,128)(2,1)}, bf16[256,768]{1,0:T(8,128)(2,1)S(1)}, u32[]{:S(2)}, u32[]{:S(2)}) %collective-permute-start) | collective-permute-done | bytes 393248 | tf_op jit(solution)/shard_map/ppermute | solution.py:190
  16.2 2.7 %collective-permute-start.5 = (bf16[256,768]{1,0:T(8,128)(2,1)S(1)}, bf16[256,768]{1,0:T(8,128)(2,1)S(1)}, u32[]{:S(2)}, u32[]{:S(2)}) collective-permute-start(bf16[256,768]{1,0:T(8,128)(2,1)S(1)} %collective-permute-done.x_ref), channel_id=1, source_target_pairs={{4,0},{5,1},{6,2},{7,3},{8,4},{9,5},{10,6},{11,7},{12,8},{13,9},{1... | collective-permute-start | bytes 1179656 | tf_op jit(solution)/shard_map/ppermute | solution.py:190
  18.8 2.4 %collective-permute-start.4 = (bf16[256,768]{1,0:T(8,128)(2,1)S(1)}, bf16[256,768]{1,0:T(8,128)(2,1)S(1)}, u32[]{:S(2)}, u32[]{:S(2)}) collective-permute-start(bf16[256,768]{1,0:T(8,128)(2,1)S(1)} %copy-done), channel_id=1, source_target_pairs={{4,0},{5,1},{6,2},{7,3},{8,4},{9,5},{10,6},{11,7},{12,8},{13,9},{1... | collective-permute-start | bytes 1179656 | tf_op jit(solution)/shard_map/ppermute | solution.py:190
  21.2 1.0 %collective-permute-done.2.x_ref = bf16[256,768]{1,0:T(8,128)(2,1)S(1)} collective-permute-done((bf16[256,768]{1,0:T(8,128)(2,1)}, bf16[256,768]{1,0:T(8,128)(2,1)S(1)}, u32[]{:S(2)}, u32[]{:S(2)}) %collective-permute-start.2) | collective-permute-done | bytes 393248 | tf_op jit(solution)/shard_map/ppermute | solution.py:190
  22.2 1.4 %collective-permute-start.7 = (bf16[256,768]{1,0:T(8,128)(2,1)S(1)}, bf16[256,768]{1,0:T(8,128)(2,1)S(1)}, u32[]{:S(2)}, u32[]{:S(2)}) collective-permute-start(bf16[256,768]{1,0:T(8,128)(2,1)S(1)} %collective-permute-done.2.x_ref), channel_id=1, source_target_pairs={{32,0},{33,1},{34,2},{35,3},{36,4},{37,5},{38,6},{39,7},{40,8},{41... | collective-permute-start | bytes 1179656 | tf_op jit(solution)/shard_map/ppermute | solution.py:190
  23.6 0.0 collective-permute-done.3.x_ref
  23.6 2.0 %collective-permute-start.6 = (bf16[256,768]{1,0:T(8,128)(2,1)S(1)}, bf16[256,768]{1,0:T(8,128)(2,1)S(1)}, u32[]{:S(2)}, u32[]{:S(2)}) collective-permute-start(bf16[256,768]{1,0:T(8,128)(2,1)S(1)} %collective-permute-done.3.x_ref), channel_id=1, source_target_pairs={{1,0},{2,1},{3,2},{0,3},{5,4},{6,5},{7,6},{4,7},{9,8},{10,9},{11,1... | collective-permute-start | bytes 1179656 | tf_op jit(solution)/shard_map/ppermute | solution.py:190
  25.6 0.0 collective-permute-done.1.x_ref
  25.6 0.0 collective-permute-start.9
  25.7 0.0 collective-permute-done.5.x_ref
  25.7 2.5 %collective-permute-start.10 = (bf16[256,768]{1,0:T(8,128)(2,1)S(1)}, bf16[256,768]{1,0:T(8,128)(2,1)S(1)}, u32[]{:S(2)}, u32[]{:S(2)}) collective-permute-start(bf16[256,768]{1,0:T(8,128)(2,1)S(1)} %collective-permute-done.5.x_ref), channel_id=1, source_target_pairs={{4,0},{5,1},{6,2},{7,3},{8,4},{9,5},{10,6},{11,7},{12,8},{13,9},{1... | collective-permute-start | bytes 1179656 | tf_op jit(solution)/shard_map/ppermute | solution.py:190
  28.2 0.2 collective-permute-done.4.x_ref
  28.3 3.0 %collective-permute-start.8 = (bf16[256,768]{1,0:T(8,128)(2,1)S(1)}, bf16[256,768]{1,0:T(8,128)(2,1)S(1)}, u32[]{:S(2)}, u32[]{:S(2)}) collective-permute-start(bf16[256,768]{1,0:T(8,128)(2,1)S(1)} %collective-permute-done.1.x_ref), channel_id=1, source_target_pairs={{1,0},{2,1},{3,2},{0,3},{5,4},{6,5},{7,6},{4,7},{9,8},{10,9},{11,1... | collective-permute-start | bytes 1179656 | tf_op jit(solution)/shard_map/ppermute | solution.py:190
  31.3 0.2 shard_map.30.refs_2_.refs_1_
  31.5 0.2 shard_map.31.refs_6_.refs_2_
  31.7 0.2 shard_map.32.refs_3_.refs_2_
  31.8 0.2 shard_map.33.refs_4_.refs_3_
  32.0 0.2 shard_map.34.refs_5_.refs_4_
  32.2 2.2 %shard_map.35.refs_10_ = f32[12,8,256]{2,1,0:T(8,128)S(1)} custom-call(s32[12]{0:T(128)S(1)} %stack.51.refs_0_, bf16[256,768]{1,0:T(8,128)(2,1)S(1)} %shard_map.28.unit_ref.refs_1_, bf16[256,768]{1,0:T(8,128)(2,1)S(1)} %shard_map.30.refs_2_.refs_1_, bf16[256,768]{1,0:T(8,128)(2,1)S(1)} %shard_map.32.refs_3_.refs_2_, ...), custom_call_target="tpu_custom_call" | custom-call | flops 1308622848 | bytes 5111808 | tf_op jit(solution)/shard_map/pallas_call | solution.py:130
  34.4 0.0 collective-permute-done.7.x_ref
  34.4 0.0 collective-permute-done.6.x_ref
  34.4 0.2 shard_map.36.refs_7_.refs_3_
  34.5 0.2 shard_map.37.refs_8_.refs_5_
  34.7 0.2 shard_map.38.refs_9_.refs_6_
  34.9 1.9 %shard_map.39.refs_5_ = f32[12,8,256]{2,1,0:T(8,128)S(1)} custom-call(s32[12]{0:T(128)S(1)} %stack.51.refs_0_, bf16[256,768]{1,0:T(8,128)(2,1)S(1)} %shard_map.28.unit_ref.refs_1_, bf16[256,768]{1,0:T(8,128)(2,1)S(1)} %shard_map.30.refs_2_.refs_1_, bf16[256,768]{1,0:T(8,128)(2,1)S(1)} %shard_map.32.refs_3_.refs_2_, ...), custom_call_target="tpu_custom_call" | custom-call | flops 1006632960 | bytes 3932160 | tf_op jit(solution)/shard_map/pallas_call | solution.py:130
  36.7 1.8 %collective-permute-done.9.x_ref = bf16[256,768]{1,0:T(8,128)(2,1)S(1)} collective-permute-done((bf16[256,768]{1,0:T(8,128)(2,1)S(1)}, bf16[256,768]{1,0:T(8,128)(2,1)S(1)}, u32[]{:S(2)}, u32[]{:S(2)}) %collective-permute-start.9) | collective-permute-done | bytes 393248 | tf_op jit(solution)/shard_map/ppermute | solution.py:190
  38.5 0.2 shard_map.40.refs_4_.refs_7_
  38.7 1.1 %shard_map.41.refs_9_ = f32[12,8,256]{2,1,0:T(8,128)S(1)} custom-call(s32[12]{0:T(128)S(1)} %stack.51.refs_0_, bf16[256,768]{1,0:T(8,128)(2,1)S(1)} %shard_map.30.refs_2_.refs_1_, bf16[256,768]{1,0:T(8,128)(2,1)S(1)} %shard_map.31.refs_6_.refs_2_, bf16[256,768]{1,0:T(8,128)(2,1)S(1)} %shard_map.36.refs_7_.refs_3_, ...), custom_call_target="tpu_custom_call" | custom-call | flops 301989888 | bytes 1179648 | tf_op jit(solution)/shard_map/pallas_call | solution.py:130
  39.8 0.0 collective-permute-done.10.x_ref
  39.8 0.2 shard_map.42.refs_8_.refs_5_
  40.0 1.5 %shard_map.43.refs_6_ = f32[12,8,256]{2,1,0:T(8,128)S(1)} custom-call(s32[12]{0:T(128)S(1)} %stack.51.refs_0_, bf16[256,768]{1,0:T(8,128)(2,1)S(1)} %shard_map.28.unit_ref.refs_1_, bf16[256,768]{1,0:T(8,128)(2,1)S(1)} %shard_map.32.refs_3_.refs_2_, bf16[256,768]{1,0:T(8,128)(2,1)S(1)} %shard_map.33.refs_4_.refs_3_, ...), custom_call_target="tpu_custom_call" | custom-call | flops 704643072 | bytes 2752512 | tf_op jit(solution)/shard_map/pallas_call | solution.py:130
  41.5 0.0 collective-permute-done.8.x_ref
  41.5 0.2 shard_map.44.refs_4_
  41.7 1.9 %shard_map.45 = (f32[8,1,256]{2,1,0:T(1,128)}, f32[1,256]{1,0:T(1,128)S(1)}, f32[1,256]{1,0:T(1,128)S(1)}, f32[1,256]{1,0:T(1,128)S(1)}) custom-call(s32[12]{0:T(128)S(1)} %stack.51.refs_0_, bf16[256,768]{1,0:T(8,128)(2,1)S(1)} %shard_map.30.refs_2_.refs_1_, bf16[256,768]{1,0:T(8,128)(2,1)S(1)} %shard_map.31.refs_6_.refs_2_, ...), custom_call_target="tpu_custom_call" | custom-call | flops 402653184 | bytes 1572864 | tf_op jit(solution)/shard_map/pallas_call | solution.py:130
  43.6 5.2 %all-to-all-start = ((f32[8,1,256]{2,1,0:T(1,128)}), f32[8,1,256]{2,1,0:T(1,128)S(1)}, u32[]{:S(2)}, u32[]{:S(2)}) async-start(f32[8,1,256]{2,1,0:T(1,128)} %get-tuple-element.47), calls=%async_computation | async-start | bytes 16384 | tf_op jit(solution)/shard_map/all_to_all | solution.py:197
  48.8 0.5 collective-permute-start.11
  49.3 4.2 %collective-permute-start.12 = (f32[1,256]{1,0:T(1,128)S(1)}, f32[1,256]{1,0:T(1,128)S(1)}, u32[]{:S(2)}, u32[]{:S(2)}) collective-permute-start(f32[1,256]{1,0:T(1,128)S(1)} %get-tuple-element.49), channel_id=1, source_target_pairs={{0,8},{1,9},{2,10},{3,11},{4,12},{5,13},{6,14},{7,15},{8,16},{9,17... | collective-permute-start | bytes 3080 | tf_op jit(solution)/shard_map/ppermute | solution.py:194
  53.5 0.5 collective-permute-start.13
  54.0 1.4 %collective-permute-done.11.refs_0_ = f32[1,256]{1,0:T(1,128)S(1)} collective-permute-done((f32[1,256]{1,0:T(1,128)S(1)}, f32[1,256]{1,0:T(1,128)S(1)}, u32[]{:S(2)}, u32[]{:S(2)}) %collective-permute-start.11) | collective-permute-done | bytes 1056 | tf_op jit(solution)/shard_map/ppermute | solution.py:194
  55.4 0.1 collective-permute-done.12.refs_1_
  55.5 2.8 %collective-permute-done.13.refs_2_ = f32[1,256]{1,0:T(1,128)S(1)} collective-permute-done((f32[1,256]{1,0:T(1,128)S(1)}, f32[1,256]{1,0:T(1,128)S(1)}, u32[]{:S(2)}, u32[]{:S(2)}) %collective-permute-start.13) | collective-permute-done | bytes 1056 | tf_op jit(solution)/shard_map/ppermute | solution.py:194
  58.2 0.0 all-to-all-done.found_ref
  58.2 0.6 shard_map.46
Async XLA Ops:
  0.0 13.1 %copy-start = (bf16[256,768]{1,0:T(8,128)(2,1)S(1)}, bf16[256,768]{1,0:T(8,128)(2,1)}, u32[]{:S(2)}) copy-start(bf16[256,768]{1,0:T(8,128)(2,1)} %x_ref.1) | copy-start | bytes 1179652
  0.0 16.2 %collective-permute-start = (bf16[256,768]{1,0:T(8,128)(2,1)}, bf16[256,768]{1,0:T(8,128)(2,1)S(1)}, u32[]{:S(2)}, u32[]{:S(2)}) collective-permute-start(bf16[256,768]{1,0:T(8,128)(2,1)} %x_ref.1), channel_id=1, source_target_pairs={{8,0},{9,1},{10,2},{11,3},{12,4},{13,5},{14,6},{15,7},{16,8},{17,9... | collective-permute-start | bytes 1179656 | tf_op jit(solution)/shard_map/ppermute | solution.py:190
  6.3 15.9 %collective-permute-start.2 = (bf16[256,768]{1,0:T(8,128)(2,1)}, bf16[256,768]{1,0:T(8,128)(2,1)S(1)}, u32[]{:S(2)}, u32[]{:S(2)}) collective-permute-start(bf16[256,768]{1,0:T(8,128)(2,1)} %x_ref.1), channel_id=1, source_target_pairs={{3,0},{0,1},{1,2},{2,3},{7,4},{4,5},{5,6},{6,7},{11,8},{8,9},{9,10... | collective-permute-start | bytes 1179656 | tf_op jit(solution)/shard_map/ppermute | solution.py:190
  7.9 15.7 %collective-permute-start.3 = (bf16[256,768]{1,0:T(8,128)(2,1)}, bf16[256,768]{1,0:T(8,128)(2,1)S(1)}, u32[]{:S(2)}, u32[]{:S(2)}) collective-permute-start(bf16[256,768]{1,0:T(8,128)(2,1)} %x_ref.1), channel_id=1, source_target_pairs={{1,0},{2,1},{3,2},{0,3},{5,4},{6,5},{7,6},{4,7},{9,8},{10,9},{11,1... | collective-permute-start | bytes 1179656 | tf_op jit(solution)/shard_map/ppermute | solution.py:190
  9.5 16.1 %collective-permute-start.1 = (bf16[256,768]{1,0:T(8,128)(2,1)}, bf16[256,768]{1,0:T(8,128)(2,1)S(1)}, u32[]{:S(2)}, u32[]{:S(2)}) collective-permute-start(bf16[256,768]{1,0:T(8,128)(2,1)} %x_ref.1), channel_id=1, source_target_pairs={{33,0},{34,1},{35,2},{32,3},{37,4},{38,5},{39,6},{36,7},{41,8},{42... | collective-permute-start | bytes 1179656 | tf_op jit(solution)/shard_map/ppermute | solution.py:190
  12.2 0.7 %copy-start.1 = (s32[256]{0:T(256)S(1)}, s32[256]{0:T(256)}, u32[]{:S(2)}) copy-start(s32[256]{0:T(256)} %param.3) | copy-start | bytes 3076
  16.2 9.5 %collective-permute-start.5 = (bf16[256,768]{1,0:T(8,128)(2,1)S(1)}, bf16[256,768]{1,0:T(8,128)(2,1)S(1)}, u32[]{:S(2)}, u32[]{:S(2)}) collective-permute-start(bf16[256,768]{1,0:T(8,128)(2,1)S(1)} %collective-permute-done.x_ref), channel_id=1, source_target_pairs={{4,0},{5,1},{6,2},{7,3},{8,4},{9,5},{10,6},{11,7},{12,8},{13,9},{1... | collective-permute-start | bytes 1179656 | tf_op jit(solution)/shard_map/ppermute | solution.py:190
  18.8 9.5 %collective-permute-start.4 = (bf16[256,768]{1,0:T(8,128)(2,1)S(1)}, bf16[256,768]{1,0:T(8,128)(2,1)S(1)}, u32[]{:S(2)}, u32[]{:S(2)}) collective-permute-start(bf16[256,768]{1,0:T(8,128)(2,1)S(1)} %copy-done), channel_id=1, source_target_pairs={{4,0},{5,1},{6,2},{7,3},{8,4},{9,5},{10,6},{11,7},{12,8},{13,9},{1... | collective-permute-start | bytes 1179656 | tf_op jit(solution)/shard_map/ppermute | solution.py:190
  22.2 12.1 %collective-permute-start.7 = (bf16[256,768]{1,0:T(8,128)(2,1)S(1)}, bf16[256,768]{1,0:T(8,128)(2,1)S(1)}, u32[]{:S(2)}, u32[]{:S(2)}) collective-permute-start(bf16[256,768]{1,0:T(8,128)(2,1)S(1)} %collective-permute-done.2.x_ref), channel_id=1, source_target_pairs={{32,0},{33,1},{34,2},{35,3},{36,4},{37,5},{38,6},{39,7},{40,8},{41... | collective-permute-start | bytes 1179656 | tf_op jit(solution)/shard_map/ppermute | solution.py:190
  23.6 10.7 %collective-permute-start.6 = (bf16[256,768]{1,0:T(8,128)(2,1)S(1)}, bf16[256,768]{1,0:T(8,128)(2,1)S(1)}, u32[]{:S(2)}, u32[]{:S(2)}) collective-permute-start(bf16[256,768]{1,0:T(8,128)(2,1)S(1)} %collective-permute-done.3.x_ref), channel_id=1, source_target_pairs={{1,0},{2,1},{3,2},{0,3},{5,4},{6,5},{7,6},{4,7},{9,8},{10,9},{11,1... | collective-permute-start | bytes 1179656 | tf_op jit(solution)/shard_map/ppermute | solution.py:190
  25.6 12.9 %collective-permute-start.9 = (bf16[256,768]{1,0:T(8,128)(2,1)S(1)}, bf16[256,768]{1,0:T(8,128)(2,1)S(1)}, u32[]{:S(2)}, u32[]{:S(2)}) collective-permute-start(bf16[256,768]{1,0:T(8,128)(2,1)S(1)} %collective-permute-done.1.x_ref), channel_id=1, source_target_pairs={{3,0},{0,1},{1,2},{2,3},{7,4},{4,5},{5,6},{6,7},{11,8},{8,9},{9,10... | collective-permute-start | bytes 1179656 | tf_op jit(solution)/shard_map/ppermute | solution.py:190
  25.7 14.1 %collective-permute-start.10 = (bf16[256,768]{1,0:T(8,128)(2,1)S(1)}, bf16[256,768]{1,0:T(8,128)(2,1)S(1)}, u32[]{:S(2)}, u32[]{:S(2)}) collective-permute-start(bf16[256,768]{1,0:T(8,128)(2,1)S(1)} %collective-permute-done.5.x_ref), channel_id=1, source_target_pairs={{4,0},{5,1},{6,2},{7,3},{8,4},{9,5},{10,6},{11,7},{12,8},{13,9},{1... | collective-permute-start | bytes 1179656 | tf_op jit(solution)/shard_map/ppermute | solution.py:190
  28.3 13.2 %collective-permute-start.8 = (bf16[256,768]{1,0:T(8,128)(2,1)S(1)}, bf16[256,768]{1,0:T(8,128)(2,1)S(1)}, u32[]{:S(2)}, u32[]{:S(2)}) collective-permute-start(bf16[256,768]{1,0:T(8,128)(2,1)S(1)} %collective-permute-done.1.x_ref), channel_id=1, source_target_pairs={{1,0},{2,1},{3,2},{0,3},{5,4},{6,5},{7,6},{4,7},{9,8},{10,9},{11,1... | collective-permute-start | bytes 1179656 | tf_op jit(solution)/shard_map/ppermute | solution.py:190
  43.6 14.7 %all-to-all-start = ((f32[8,1,256]{2,1,0:T(1,128)}), f32[8,1,256]{2,1,0:T(1,128)S(1)}, u32[]{:S(2)}, u32[]{:S(2)}) async-start(f32[8,1,256]{2,1,0:T(1,128)} %get-tuple-element.47), calls=%async_computation | async-start | bytes 16384 | tf_op jit(solution)/shard_map/all_to_all | solution.py:197
  48.8 6.6 %collective-permute-start.11 = (f32[1,256]{1,0:T(1,128)S(1)}, f32[1,256]{1,0:T(1,128)S(1)}, u32[]{:S(2)}, u32[]{:S(2)}) collective-permute-start(f32[1,256]{1,0:T(1,128)S(1)} %get-tuple-element.48), channel_id=1, source_target_pairs={{0,12},{1,13},{2,14},{3,15},{4,16},{5,17},{6,18},{7,19},{8,20},{9,... | collective-permute-start | bytes 3080 | tf_op jit(solution)/shard_map/ppermute | solution.py:194
  49.3 6.2 %collective-permute-start.12 = (f32[1,256]{1,0:T(1,128)S(1)}, f32[1,256]{1,0:T(1,128)S(1)}, u32[]{:S(2)}, u32[]{:S(2)}) collective-permute-start(f32[1,256]{1,0:T(1,128)S(1)} %get-tuple-element.49), channel_id=1, source_target_pairs={{0,8},{1,9},{2,10},{3,11},{4,12},{5,13},{6,14},{7,15},{8,16},{9,17... | collective-permute-start | bytes 3080 | tf_op jit(solution)/shard_map/ppermute | solution.py:194
  53.5 4.8 %collective-permute-start.13 = (f32[1,256]{1,0:T(1,128)S(1)}, f32[1,256]{1,0:T(1,128)S(1)}, u32[]{:S(2)}, u32[]{:S(2)}) collective-permute-start(f32[1,256]{1,0:T(1,128)S(1)} %get-tuple-element.50), channel_id=1, source_target_pairs={{0,4},{1,5},{2,6},{3,7},{4,8},{5,9},{6,10},{7,11},{8,12},{9,13},{1... | collective-permute-start | bytes 3080 | tf_op jit(solution)/shard_map/ppermute | solution.py:194
